TPU v7x, 32 devices: a whole 2x2x4 slice. The times are simulated.
32 devices in a mesh: sub: 16 (over z, y, x), rng: 2 (over core).
Axes of the slice: x: 2, y: 2, z: 4, core: 2. Of those that a mesh axis runs over, the one named last changes fastest.
Arguments:
- raw_echoes: bfloat16 [2048, 2, 16384], P('sub', None, 'rng'), may hold values from -6 to 6
- chirp_replica: bfloat16 [2, 512], replicated, may hold values from -0.1875 to 0.1875
- steering: bfloat16 [16, 2, 128, 128], P('sub'), may hold values from -0.375 to 0.375
- band_start: int32 [4, 16, 2, 128], P(None, 'sub'), may hold values from 0 to 120
- band_coef: bfloat16 [4, 16, 2, 2, 8, 128], P(None, 'sub'), may hold values from -1 to 1
- phase_rate: float32 [4, 16, 128], P(None, 'sub'), may hold values from -8 to 8
- range_map: bfloat16 [2, 8192, 256], P(None, 'rng'), may hold values from -0.0625 to 0.0625
- slot_maps: bfloat16 [512, 2, 32, 128], P(('sub', 'rng')), may hold values from -0.09375 to 0.09375
- coverage: int32 [512, 1], P(('sub', 'rng')), may hold values from 0 to 31, as said below
Outputs:
- ground_tiles: float32 [32, 2, 32, 256], P(('sub', 'rng'))
Inputs may be any that keep to these rules, and one draw needn't show every extreme that they name: `coverage`: within the rows of one device (aligned blocks of 16 rows) no tile is named more than 2 times; in every block one tile is named exactly 2 times.
All inputs are finite; a program needn't handle non-finite values.
Results may differ from a plain program's by a relative error of at most 0.012.
Values may be sent and summed in bfloat16 or wider, within the bound.
A program may use at most 128 MiB of HBM per device.

v0:
```python
import math

import jax
import jax.numpy as jnp
from jax import lax
from jax.sharding import PartitionSpec as P

CAP = 2


def from_behind(value, axis, steps):
    count = lax.axis_size(axis)
    initial, last = (max(0, -steps), min(count, count - steps))
    return lax.ppermute(value, axis, [(source, source + steps) for source in range(initial, last)])


def swapped(value, axis, distance):
    mask = 2**distance
    pairs = [(source, source ^ mask) for source in range(lax.axis_size(axis))]
    return lax.ppermute(value, axis, pairs)


def toeplitz_taps(replica, quarter, window_width):
    tap_count = replica.shape[1]
    period = window_width + 2
    padded = jnp.concatenate([replica, jnp.zeros((2, period - tap_count), replica.dtype)], axis=1)
    repeated = jnp.tile(padded, (1, quarter + 1))[:, : quarter * window_width]
    return jnp.transpose(repeated.reshape(2, quarter, window_width), (0, 2, 1))


def band_matrix(coef_pair, start_rows):
    beams = start_rows.shape[0]
    offset_grid = lax.iota(jnp.int32, beams)[None, :] - start_rows[:, None]
    total = jnp.zeros((2, beams, beams), jnp.float32)
    for tap_index in range(coef_pair.shape[1]):
        total = total + jnp.where(
            (offset_grid == tap_index)[None],
            coef_pair[:, tap_index, :, None].astype(jnp.float32),
            0.0,
        )
    return total.astype(jnp.bfloat16)


def complex_apply(matrix, field):
    products = jnp.einsum("cbe,der->cdbr", matrix, field, preferred_element_type=jnp.float32)
    return (products[0, 0] - products[1, 1], products[0, 1] + products[1, 0])


def shards(
    raw_echoes,
    chirp_replica,
    steering,
    band_start,
    band_coef,
    phase_rate,
    range_map,
    slot_maps,
    coverage,
):
    pulses = raw_echoes.shape[0]
    range_len = raw_echoes.shape[2]
    tap_count = chirp_replica.shape[1]
    quarter = tap_count // 4
    stride = 2 * quarter
    window_count = range_len // stride
    following = from_behind(raw_echoes[:, :, :tap_count], "rng", -1)
    extended = jnp.concatenate([raw_echoes, following], axis=2)
    blocks = extended.reshape(pulses, 2, window_count + 2, stride)
    windows = jnp.concatenate(
        [blocks[:, :, :window_count], blocks[:, :, 1 : window_count + 1], blocks[:, :, 2:]], axis=3
    )
    kernel = toeplitz_taps(chirp_replica, quarter, 3 * stride)
    products = jnp.einsum("pcnw,ewq->pcenq", windows, kernel, preferred_element_type=jnp.float32)
    real_part = products[:, 0, 0] + products[:, 1, 1]
    imag_part = products[:, 1, 0] - products[:, 0, 1]
    compressed = (
        jnp.stack([real_part, imag_part], axis=1)
        .reshape(pulses, 2, window_count * quarter)
        .astype(jnp.bfloat16)
    )
    steer_products = jnp.einsum(
        "cbp,pdr->cdbr", steering[0], compressed, preferred_element_type=jnp.float32
    )
    polar_image = jnp.stack(
        [steer_products[0, 0] - steer_products[1, 1], steer_products[0, 1] + steer_products[1, 0]]
    ).astype(jnp.bfloat16)
    bins_dev = polar_image.shape[2]
    bin_index = (lax.axis_index("rng") * bins_dev + lax.iota(jnp.int32, bins_dev)).astype(
        jnp.float32
    )
    for section_bit in range(band_coef.shape[0]):
        partner = swapped(polar_image, "sub", section_bit)
        own_matrix = band_matrix(band_coef[section_bit, 0, 0], band_start[section_bit, 0, 0])
        partner_matrix = band_matrix(band_coef[section_bit, 0, 1], band_start[section_bit, 0, 1])
        own_real, own_imag = complex_apply(own_matrix, polar_image)
        part_real, part_imag = complex_apply(partner_matrix, partner)
        angle = (
            phase_rate[section_bit, 0][:, None] * bin_index[None, :] * (2.0 * math.pi / bins_dev)
        )
        cosine = jnp.cos(angle)
        sine = jnp.sin(angle)
        turned_real = part_real * cosine - part_imag * sine
        turned_imag = part_real * sine + part_imag * cosine
        polar_image = jnp.stack([own_real + turned_real, own_imag + turned_imag]).astype(
            jnp.bfloat16
        )
    basis_products = jnp.einsum(
        "cbr,drt->cdbt", polar_image, range_map, preferred_element_type=jnp.float32
    )
    tile_basis = jnp.stack(
        [basis_products[0, 0] - basis_products[1, 1], basis_products[0, 1] + basis_products[1, 0]]
    ).astype(jnp.bfloat16)
    slot_count = slot_maps.shape[0]
    tile_rows = slot_maps.shape[2]
    tile_cols = range_map.shape[2]
    slot_products = jnp.einsum(
        "kcab,dbt->kcdat", slot_maps, tile_basis, preferred_element_type=jnp.float32
    )
    flat_parts = jnp.stack(
        [
            slot_products[:, 0, 0] - slot_products[:, 1, 1],
            slot_products[:, 0, 1] + slot_products[:, 1, 0],
        ],
        axis=1,
    ).reshape(slot_count, 2 * tile_rows * tile_cols)
    targets = coverage[:, 0]
    owners = lax.axis_size(("sub", "rng"))
    slot_ids = lax.iota(jnp.int32, slot_count)
    same_tile = (targets[:, None] == targets[None, :]) & (slot_ids[:, None] > slot_ids[None, :])
    slot_rank = jnp.sum(same_tile.astype(jnp.int32), axis=1)
    position = targets * CAP + slot_rank
    select = (lax.iota(jnp.int32, owners * CAP)[:, None] == position[None, :]).astype(jnp.float32)
    outgoing = jnp.dot(
        select, flat_parts, precision=lax.Precision.HIGHEST, preferred_element_type=jnp.float32
    )
    outgoing = outgoing.reshape(owners, CAP * 2 * tile_rows * tile_cols)
    received = lax.all_to_all(outgoing, ("sub", "rng"), split_axis=0, concat_axis=0, tiled=True)
    own_tile = jnp.sum(received.reshape(owners * CAP, 2 * tile_rows * tile_cols), axis=0)
    return own_tile.reshape(1, 2, tile_rows, tile_cols)


def solution(mesh):
    in_specs = (
        P("sub", None, "rng"),
        P(),
        P("sub", None, None, None),
        P(None, "sub", None, None),
        P(None, "sub", None, None, None, None),
        P(None, "sub", None),
        P(None, "rng", None),
        P(("sub", "rng"), None, None, None),
        P(("sub", "rng"), None),
    )
    out_specs = P(("sub", "rng"), None, None, None)
    return jax.shard_map(shards, mesh=mesh, in_specs=in_specs, out_specs=out_specs, check_vma=False)
```

profile of v0, /device:TPU:0, one launch (start us, length us, event | category | flops | bytes accessed | tf_op | source)
XLA Modules:
  0.0 474.2 jit_solution(3187577478573095639)
XLA Ops:
  0.0 11.2 %copy.66 = bf16[128,2,8192]{0,2,1:T(8,128)(2,1)} copy(bf16[128,2,8192]{2,1,0:T(2,128)(2,1)} %param.9) | data formatting | bytes 8388608 | tf_op args[0]
  11.2 1.0 slice.549
  12.2 1.3 collective-permute-start
  13.6 1.1 tile.10
  14.7 0.9 collective-permute-done
  15.6 5.7 %pad_maximum_fusion = bf16[128,2,8704]{0,2,1:T(8,128)(2,1)S(1)} fusion(bf16[128,2,512]{0,2,1:T(8,128)(2,1)S(1)} %collective-permute-done, bf16[128,2,8192]{0,2,1:T(8,128)(2,1)} %copy.66), kind=kLoop, calls=%fused_computation.15 | loop fusion | flops 8912896 | bytes 8912896 | tf_op jit(solution)/shard_map/concatenate | solution.py:67
  21.4 4.8 %fusion.314 = (bf16[128,2,32,256]{0,3,2,1:T(8,128)(2,1)}, bf16[128,2,32,256]{0,3,2,1:T(8,128)(2,1)}, bf16[128,2,32,256]{0,3,2,1:T(8,128)(2,1)}) fusion(bf16[128,2,34,256]{0,3,2,1:T(8,128)(2,1)S(1)} %bitcast.392), kind=kLoop, calls=%fused_computation.461 | loop fusion | bytes 25165824 | tf_op jit(solution)/shard_map/slice | solution.py:70
  26.1 6.3 %copy.107 = bf16[128,2,32,256]{3,0,2,1:T(8,128)(2,1)} copy(bf16[128,2,32,256]{0,3,2,1:T(8,128)(2,1)} %get-tuple-element.15) | data formatting | bytes 8388608
  32.4 6.4 %copy.108 = bf16[128,2,32,256]{3,0,2,1:T(8,128)(2,1)} copy(bf16[128,2,32,256]{0,3,2,1:T(8,128)(2,1)} %get-tuple-element.16) | data formatting | bytes 8388608
  38.8 6.4 %copy.109 = bf16[128,2,32,256]{3,0,2,1:T(8,128)(2,1)} copy(bf16[128,2,32,256]{0,3,2,1:T(8,128)(2,1)} %get-tuple-element.17) | data formatting | bytes 8388608
  45.2 7.1 %fusion.7 = f32[128,2,2,32,128]{0,4,3,1,2:T(8,128)S(1)} fusion(bf16[128,2,32,256]{3,0,2,1:T(8,128)(2,1)} %copy.109, bf16[128,2,32,256]{3,0,2,1:T(8,128)(2,1)} %copy.108, bf16[128,2,32,256]{3,0,2,1:T(8,128)(2,1)} %copy.107, bf16[1,2,128,768]{3,1,2,0:T(2,128)(2,1)S(1)} %bitcast.397), kind=kOutput, calls=%fused_computation.18 | convolution fusion | flops 3258974208 | bytes 21364736 | tf_op jit(solution)/shard_map/pcnw,ewq->pcenq/dot_general | solution.py:73
  52.3 0.0 copy-start.2
  52.3 0.9 fusion.45
  53.2 1.2 convolution_bitcast_fusion.8
  54.4 0.2 fusion.69
  54.7 0.2 fusion.70
  54.9 0.0 copy-start.6
  54.9 0.0 copy-start.4
  54.9 0.0 copy-start.3
  54.9 1.5 pad_maximum_fusion.1
  56.4 2.9 collective-permute-start.1
  59.4 0.1 fusion.234
  59.6 0.2 fusion.194
  59.9 1.6 convolution_bitcast_fusion.7
  61.4 44.4 %collective-permute-done.1 = bf16[2,128,4096]{1,2,0:T(8,128)(2,1)} collective-permute-done((bf16[2,128,4096]{1,2,0:T(8,128)(2,1)}, bf16[2,128,4096]{1,2,0:T(8,128)(2,1)}, u32[]{:S(2)}, u32[]{:S(2)}) %collective-permute-start.1) | collective-permute-done | bytes 2097184 | tf_op jit(solution)/shard_map/ppermute | solution.py:20
  105.8 3.1 convolution_bitcast_fusion.6
  109.0 10.1 %fusion.40 = (bf16[1,128,4096]{1,2,0:T(8,128)(2,1)S(1)}, bf16[1,128,4096]{1,2,0:T(8,128)(2,1)S(1)}) fusion(f32[2,2,128,4096]{2,3,0,1:T(8,128)S(1)} %convolution_bitcast_fusion.7, f32[4096]{0:T(1024)S(1)} %add_convert_fusion.8, f32[128]{0:T(128)S(1)} %get-tuple-element.102, f32[2,2,128,4096]{2,3,1,0:T(8,128)S(1)} %convolution_bitcast_fusion.6), kind=kLoop, calls=%fused_computation.67 | loop fusion | flops 8388608 | bytes 18891264 | tf_op jit(solution)/shard_map/convert.74
  119.1 0.2 pad_maximum_fusion.2
  119.3 1.8 collective-permute-start.2
  121.2 0.2 fusion.162
  121.4 1.6 convolution_bitcast_fusion.5
  123.0 43.8 %collective-permute-done.2 = bf16[2,128,4096]{1,2,0:T(8,128)(2,1)S(1)} collective-permute-done((bf16[2,128,4096]{1,2,0:T(8,128)(2,1)S(1)}, bf16[2,128,4096]{1,2,0:T(8,128)(2,1)S(1)}, u32[]{:S(2)}, u32[]{:S(2)}) %collective-permute-start.2) | collective-permute-done | bytes 2097184 | tf_op jit(solution)/shard_map/ppermute | solution.py:20
  166.8 1.6 convolution_bitcast_fusion.4
  168.3 10.0 %fusion.31 = (bf16[1,128,4096]{1,2,0:T(8,128)(2,1)S(1)}, bf16[1,128,4096]{1,2,0:T(8,128)(2,1)S(1)}) fusion(f32[2,2,128,4096]{2,3,1,0:T(8,128)S(1)} %convolution_bitcast_fusion.5, f32[128]{0:T(128)S(1)} %get-tuple-element.101, f32[4096]{0:T(1024)S(1)} %add_convert_fusion.8, f32[2,2,128,4096]{2,3,1,0:T(8,128)S(1)} %convolution_bitcast_fusion.4), kind=kLoop, calls=%fused_computation.54 | loop fusion | flops 8388608 | bytes 18891264 | tf_op jit(solution)/shard_map/convert.72
  178.3 0.2 pad_maximum_fusion.3
  178.5 1.6 collective-permute-start.3
  180.1 0.2 fusion.130
  180.4 1.6 convolution_bitcast_fusion.3
  181.9 43.2 %collective-permute-done.3 = bf16[2,128,4096]{1,2,0:T(8,128)(2,1)S(1)} collective-permute-done((bf16[2,128,4096]{1,2,0:T(8,128)(2,1)S(1)}, bf16[2,128,4096]{1,2,0:T(8,128)(2,1)S(1)}, u32[]{:S(2)}, u32[]{:S(2)}) %collective-permute-start.3) | collective-permute-done | bytes 2097184 | tf_op jit(solution)/shard_map/ppermute | solution.py:20
  225.1 1.6 convolution_bitcast_fusion.2
  226.7 10.0 %fusion.23 = (bf16[1,128,4096]{1,2,0:T(8,128)(2,1)S(1)}, bf16[1,128,4096]{1,2,0:T(8,128)(2,1)S(1)}) fusion(f32[2,2,128,4096]{2,3,1,0:T(8,128)S(1)} %convolution_bitcast_fusion.3, f32[128]{0:T(128)S(1)} %get-tuple-element.103, f32[4096]{0:T(1024)S(1)} %add_convert_fusion.8, f32[2,2,128,4096]{2,3,1,0:T(8,128)S(1)} %convolution_bitcast_fusion.2), kind=kLoop, calls=%fused_computation.42 | loop fusion | flops 8388608 | bytes 18891264 | tf_op jit(solution)/shard_map/convert.70
  236.7 0.2 pad_maximum_fusion.4
  236.9 2.2 collective-permute-start.4
  239.1 0.2 convert_reduce_fusion
  239.3 0.1 fusion.114
  239.5 1.6 convolution_bitcast_fusion.1
  241.0 87.3 %collective-permute-done.4 = bf16[2,128,4096]{1,2,0:T(8,128)(2,1)S(1)} collective-permute-done((bf16[2,128,4096]{1,2,0:T(8,128)(2,1)S(1)}, bf16[2,128,4096]{1,2,0:T(8,128)(2,1)S(1)}, u32[]{:S(2)}, u32[]{:S(2)}) %collective-permute-start.4) | collective-permute-done | bytes 2097184 | tf_op jit(solution)/shard_map/ppermute | solution.py:20
  328.4 1.6 convolution_bitcast_fusion
  329.9 0.0 copy-start.7
  329.9 10.2 %fusion.15 = (bf16[1,128,4096]{1,2,0:T(8,128)(2,1)S(1)}, bf16[1,128,4096]{1,2,0:T(8,128)(2,1)S(1)}) fusion(f32[2,2,128,4096]{2,3,1,0:T(8,128)S(1)} %convolution_bitcast_fusion.1, f32[128]{0:T(128)S(1)} %get-tuple-element.100, f32[4096]{0:T(1024)S(1)} %add_convert_fusion.8, f32[2,2,128,4096]{2,3,1,0:T(8,128)S(1)} %convolution_bitcast_fusion), kind=kLoop, calls=%fused_computation.30 | loop fusion | flops 8388608 | bytes 18891264 | tf_op jit(solution)/shard_map/convert.68
  340.1 1.3 fusion.66
  341.5 0.4 convolution_bitcast_fusion.9
  341.9 0.1 fusion.71
  342.0 0.1 fusion.73
  342.0 0.1 pad_maximum_fusion.5
  342.2 0.1 copy.84
  342.3 0.6 copy.117
  342.9 3.8 fusion.299
  346.7 7.6 %all_to_all.8 = f32[32,1,32768]{2,1,0:T(1,128)} reshape(f32[64,16384]{1,0:T(8,128)} %fusion.299) | data formatting | bytes 8388608 | tf_op jit(solution)/shard_map/all_to_all | solution.py:137
  354.3 98.7 %all_to_all.10 = f32[32,1,32768]{2,1,0:T(1,128)} all-to-all(f32[32,1,32768]{2,1,0:T(1,128)} %all_to_all.8), channel_id=1, replica_groups=mesh['sub'=16,'rng'=2] {'sub','rng'}, dimensions={0} | all-to-all | bytes 8388608 | tf_op jit(solution)/shard_map/all_to_all | solution.py:137
  453.0 13.0 %reduce = f32[32,32768]{1,0:T(8,128)} reduce(f32[32,1,32768]{2,1,0:T(1,128)} %all_to_all.10, f32[]{:T(128)} %constant.38), dimensions={1}, to_apply=%all_to_all.7.reduce_sub_computation | reduce | bytes 8388612 | tf_op jit(solution)/shard_map/all_to_all | solution.py:137
  466.1 5.0 %reshape.2906 = f32[64,16384]{1,0:T(8,128)} reshape(f32[32,32768]{1,0:T(8,128)} %reduce) | data formatting | bytes 8388608 | tf_op jit(solution)/shard_map/reshape | solution.py:138
  471.1 2.5 reduce_sum.19
  473.6 0.6 reshape.2907
  (27 shorter events, 0.2 us)
Async XLA Ops:
  0.0 341.5 %copy-start = (bf16[16,2,32,128]{3,2,1,0:T(8,128)(2,1)S(1)}, bf16[16,2,32,128]{3,2,1,0:T(8,128)(2,1)}, u32[]{:S(2)}) copy-start(bf16[16,2,32,128]{3,2,1,0:T(8,128)(2,1)} %param.16) | copy-start | bytes 786436
  0.0 13.5 %copy-start.5 = (bf16[2,512]{1,0:T(2,128)(2,1)S(1)}, bf16[2,512]{1,0:T(2,128)(2,1)}, u32[]{:S(2)}) copy-start(bf16[2,512]{1,0:T(2,128)(2,1)} %param.10) | copy-start | bytes 6148
  12.2 3.4 collective-permute-start
  14.7 6.7 %copy-start.1 = (bf16[2,99330]{1,0:T(2,128)(2,1)}, bf16[2,99330]{1,0:T(2,128)(2,1)S(1)}, u32[]{:S(2)}) copy-start(bf16[2,99330]{1,0:T(2,128)(2,1)S(1)} %tile.10) | copy-start | bytes 1191964
  38.8 6.4 %slice-start = ((bf16[2,99330]{1,0:T(2,128)(2,1)}), bf16[2,98304]{1,0:T(2,128)(2,1)S(1)}, s32[]{:S(2)}) async-start(bf16[2,99330]{1,0:T(2,128)(2,1)} %copy-done.1), calls=%async_computation.1 | async-start | bytes 786432 | tf_op jit(solution)/shard_map/slice | solution.py:27
  52.3 0.9 copy-start.2
  54.9 4.5 copy-start.6
  54.9 4.5 copy-start.4
  54.9 4.5 copy-start.3
  56.4 49.4 %collective-permute-start.1 = (bf16[2,128,4096]{1,2,0:T(8,128)(2,1)}, bf16[2,128,4096]{1,2,0:T(8,128)(2,1)}, u32[]{:S(2)}, u32[]{:S(2)}) collective-permute-start(bf16[2,128,4096]{1,2,0:T(8,128)(2,1)} %pad_maximum_fusion.1), channel_id=1, source_target_pairs={{0,2},{2,0},{4,6},{6,4},{8,10},{10,8},{12,14},{14,12},{16,18},{18,... | collective-permute-start | bytes 6291464 | tf_op jit(solution)/shard_map/ppermute | solution.py:20
  119.3 47.5 %collective-permute-start.2 = (bf16[2,128,4096]{1,2,0:T(8,128)(2,1)S(1)}, bf16[2,128,4096]{1,2,0:T(8,128)(2,1)S(1)}, u32[]{:S(2)}, u32[]{:S(2)}) collective-permute-start(bf16[2,128,4096]{1,2,0:T(8,128)(2,1)S(1)} %pad_maximum_fusion.2), channel_id=1, source_target_pairs={{0,4},{2,6},{4,0},{6,2},{8,12},{10,14},{12,8},{14,10},{16,20},{18,... | collective-permute-start | bytes 6291464 | tf_op jit(solution)/shard_map/ppermute | solution.py:20
  178.5 46.6 %collective-permute-start.3 = (bf16[2,128,4096]{1,2,0:T(8,128)(2,1)S(1)}, bf16[2,128,4096]{1,2,0:T(8,128)(2,1)S(1)}, u32[]{:S(2)}, u32[]{:S(2)}) collective-permute-start(bf16[2,128,4096]{1,2,0:T(8,128)(2,1)S(1)} %pad_maximum_fusion.3), channel_id=1, source_target_pairs={{0,8},{2,10},{4,12},{6,14},{8,0},{10,2},{12,4},{14,6},{16,24},{18,... | collective-permute-start | bytes 6291464 | tf_op jit(solution)/shard_map/ppermute | solution.py:20
  236.6 2.5 copy-start.8
  236.9 91.5 %collective-permute-start.4 = (bf16[2,128,4096]{1,2,0:T(8,128)(2,1)S(1)}, bf16[2,128,4096]{1,2,0:T(8,128)(2,1)S(1)}, u32[]{:S(2)}, u32[]{:S(2)}) collective-permute-start(bf16[2,128,4096]{1,2,0:T(8,128)(2,1)S(1)} %pad_maximum_fusion.4), channel_id=1, source_target_pairs={{0,16},{2,18},{4,20},{6,22},{8,24},{10,26},{12,28},{14,30},{16,0},... | collective-permute-start | bytes 6291464 | tf_op jit(solution)/shard_map/ppermute | solution.py:20
  329.9 10.2 %copy-start.7 = (bf16[2,4096,256]{2,1,0:T(8,128)(2,1)S(1)}, bf16[2,4096,256]{2,1,0:T(8,128)(2,1)}, u32[]{:S(2)}) copy-start(bf16[2,4096,256]{2,1,0:T(8,128)(2,1)} %param.15) | copy-start | bytes 12582916
where the time goes:
time: 475 us; the launch traced here: 474 us
  waiting for transfers between devices  220 us (46%)
  blocking collectives  98.7 us (21%)
  other arithmetic  66.4 us (14%)
  local copies, waits for them, and re-layouts  51.2 us (11%)
  matrix products  27.9 us (6%)
  starting transfers between devices  9.89 us (2%)
    ppermute x4, waiting for transfers between devices, swapped(): return lax.ppermute(value, axis, pairs)  219 us
    all_to_all x1, blocking collectives, shards(): lax.all_to_all(outgoing, ('sub', 'rng'), split_axis=0, concat_axis=0, til...  98.7 us
    another operation x5, other arithmetic  41.1 us
    unnamed x23, local copies, waits for them, and re-layouts  30.9 us
    dot_general x8, matrix products, complex_apply(): jnp.einsum('cbe,der->cdbr', matrix, field, preferred_element_type=jnp.flo...  14.1 us
    all_to_all x1, other arithmetic, shards(): lax.all_to_all(outgoing, ('sub', 'rng'), split_axis=0, concat_axis=0, til...  13 us
  transfers between devices with their start and end apart: 5, of which 5 were waited for; matrix products, arithmetic and copies ran while one was open for 2% of the time, Pallas kernels for 0%

commit v1 on v0

v1 whole, which is shorter than its diff:
```python
import functools
import math

import jax
import jax.numpy as jnp
from jax import lax
from jax.experimental import pallas as pl
from jax.experimental.pallas import tpu as pltpu
from jax.sharding import PartitionSpec as P

LANES = 128
F32 = jnp.float32
BF16 = jnp.bfloat16
SLOT_BLOCK = 16


def mm(a, b):
    return jnp.dot(a, b, preferred_element_type=F32)


def from_behind(value, axis, steps):
    count = lax.axis_size(axis)
    initial, last = (max(0, -steps), min(count, count - steps))
    return lax.ppermute(value, axis, [(source, source + steps) for source in range(initial, last)])


def toeplitz_taps(replica, quarter, window_width):
    tap_count = replica.shape[1]
    period = window_width + 2
    padded = jnp.concatenate([replica, jnp.zeros((2, period - tap_count), replica.dtype)], axis=1)
    repeated = jnp.tile(padded, (1, quarter + 1))[:, : quarter * window_width]
    return jnp.transpose(repeated.reshape(2 * quarter, window_width))


def front_kernel(steer_ref, taps_ref, raw_ref, next_ref, halo_ref, out_ref):
    beams = out_ref.shape[0] // 2
    quarter = taps_ref.shape[1] // 2
    last = pl.program_id(0) == pl.num_programs(0) - 1
    steer = steer_ref[...]
    after = jnp.where(last, halo_ref[...], next_ref[...])
    here = mm(steer, raw_ref[...]).astype(BF16)
    beyond = mm(steer, after).astype(BF16)
    field = jnp.concatenate([here, beyond], axis=1)
    width = taps_ref.shape[0]
    stride = 2 * quarter
    for n in range(raw_ref.shape[1] // stride):
        both = mm(field[:, n * stride : n * stride + width], taps_ref[...])
        cols = pl.ds(n * quarter, quarter)
        out_ref[:beams, cols] = (both[:beams, :quarter] + both[beams:, quarter:]).astype(BF16)
        out_ref[beams:, cols] = (both[beams:, :quarter] - both[:beams, quarter:]).astype(BF16)


def front(steer, taps, raw, halo):
    rows, length = raw.shape
    reach = halo.shape[1]
    chunk = 2 * reach
    steps = length // chunk
    ahead = chunk // reach
    return pl.pallas_call(
        front_kernel,
        grid=(steps,),
        in_specs=[
            pl.BlockSpec(steer.shape, lambda i: (0, 0)),
            pl.BlockSpec(taps.shape, lambda i: (0, 0)),
            pl.BlockSpec((rows, chunk), lambda i: (0, i)),
            pl.BlockSpec(
                (rows, reach), lambda i: (0, jnp.minimum(ahead * (i + 1), ahead * steps - 1))
            ),
            pl.BlockSpec(halo.shape, lambda i: (0, 0)),
        ],
        out_specs=pl.BlockSpec((steer.shape[0], chunk // 2), lambda i: (0, i)),
        out_shape=jax.ShapeDtypeStruct((steer.shape[0], length // 2), BF16),
        compiler_params=pltpu.CompilerParams(vmem_limit_bytes=40 * 1024 * 1024),
        cost_estimate=pl.CostEstimate(
            flops=8 * 10**9, bytes_accessed=7 * 10**6, transcendentals=0
        ),
        name="front",
    )(steer, taps, raw, raw, halo)


def top_bit(e):
    return e.bit_length() - 1


def own_list(sections):
    return [
        (s, e) for e in range(2**sections) for s in range(top_bit(e) + 1, sections)
    ]


def matrices_kernel(sections, taps, pick_ref, data_ref, turn_ref, own_ref, built):
    beams = data_ref.shape[4]
    nodes = 2**sections
    rows = lax.broadcasted_iota(jnp.int32, (beams, beams), 0).astype(F32)

    def build(m, carry):
        at = (pick_ref[3 * m], pick_ref[3 * m + 1], pick_ref[3 * m + 2])
        offset = rows - data_ref[at + (slice(2 * taps, 2 * taps + 1), slice(None))]
        real = jnp.zeros((beams, beams), F32)
        imag = jnp.zeros((beams, beams), F32)
        for t in range(taps):
            hit = offset == t
            real = jnp.where(hit, data_ref[at + (slice(t, t + 1), slice(None))], real)
            imag = jnp.where(
                hit, data_ref[at + (slice(taps + t, taps + t + 1), slice(None))], imag
            )
        built[m, :beams, :beams] = real.astype(BF16)
        built[m, beams:, beams:] = real.astype(BF16)
        built[m, :beams, beams:] = imag.astype(BF16)
        built[m, beams:, :beams] = (-imag).astype(BF16)
        return carry

    lax.fori_loop(0, built.shape[0], build, 0)
    place = {key: nodes - 1 + n for n, key in enumerate(own_list(sections))}
    for e in range(nodes):
        chain = None
        for s in range(top_bit(e) + 1, sections):
            child = e | 2**s
            partner = built[child - 1]
            turned = partner.astype(F32) if chain is None else mm(chain, partner)
            turn_ref[child - 1] = turned.T.astype(BF16)
            own = built[place[(s, e)]]
            chain = own if chain is None else mm(chain, own).astype(BF16)
        if chain is not None:
            own_ref[e] = chain.astype(F32).T.astype(BF16)


def matrices(data, place, sections, taps):
    nodes = 2**sections
    beams = data.shape[4]
    wanted = [(e, top_bit(e), 1) for e in range(1, nodes)]
    wanted += [(e, s, 0) for s, e in own_list(sections)]
    picks = jnp.stack([jnp.stack([place ^ e, place * 0 + s, place * 0 + j]) for e, s, j in wanted])
    return pl.pallas_call(
        functools.partial(matrices_kernel, sections, taps),
        grid_spec=pltpu.PrefetchScalarGridSpec(
            num_scalar_prefetch=1,
            grid=(1,),
            in_specs=[pl.BlockSpec(data.shape, lambda i, p: (0,) * 5)],
            out_specs=(
                pl.BlockSpec((nodes - 1, 2 * beams, 2 * beams), lambda i, p: (0, 0, 0)),
                pl.BlockSpec((nodes // 2, 2 * beams, 2 * beams), lambda i, p: (0, 0, 0)),
            ),
            scratch_shapes=[pltpu.VMEM((len(wanted), 2 * beams, 2 * beams), BF16)],
        ),
        out_shape=(
            jax.ShapeDtypeStruct((nodes - 1, 2 * beams, 2 * beams), BF16),
            jax.ShapeDtypeStruct((nodes // 2, 2 * beams, 2 * beams), BF16),
        ),
        compiler_params=pltpu.CompilerParams(vmem_limit_bytes=40 * 1024 * 1024),
        cost_estimate=pl.CostEstimate(
            flops=5 * 10**9, bytes_accessed=5 * 10**6, transcendentals=0
        ),
        name="matrices",
    )(picks.reshape(-1), data)


def tree_kernel(
    sections, polar_ref, map_ref, turn_ref, own_ref, fine_ref, coarse_ref, out_ref, field, total
):
    step = pl.program_id(0)
    beams = polar_ref.shape[0] // 2
    width = polar_ref.shape[1]
    cols = map_ref.shape[2]
    nodes = 2**sections

    @pl.when(step == 0)
    def _():
        total[...] = jnp.zeros_like(total)

    def project(e, value):
        total[e, :, :cols] += mm(value, map_ref[0])
        total[e, :, cols:] += mm(value, map_ref[1])

    field[0] = polar_ref[...]
    project(0, polar_ref[...])
    for e in range(1, nodes):
        parent = e ^ (2 ** top_bit(e))
        merged = mm(turn_ref[e - 1], field[parent])
        fine_cos, fine_sin = fine_ref[e - 1, 0], fine_ref[e - 1, 1]
        for j in range(width // LANES):
            at = slice(j * LANES, (j + 1) * LANES)
            c = coarse_ref[0, e - 1, 0, :, j : j + 1]
            s = coarse_ref[0, e - 1, 1, :, j : j + 1]
            cosine = fine_cos * c - fine_sin * s
            sine = fine_cos * s + fine_sin * c
            real, imag = merged[:beams, at], merged[beams:, at]
            field[e, :beams, at] = (real * cosine - imag * sine).astype(BF16)
            field[e, beams:, at] = (real * sine + imag * cosine).astype(BF16)
        project(e, field[e])

    @pl.when(step == pl.num_programs(0) - 1)
    def _():
        for e in range(nodes):
            real = total[e, :beams, :cols] - total[e, beams:, cols:]
            imag = total[e, :beams, cols:] + total[e, beams:, :cols]
            basis = jnp.concatenate([real, imag], axis=0).astype(BF16)
            if e < nodes // 2:
                basis = mm(own_ref[e], basis).astype(BF16)
            out_ref[e] = basis


def tree(polar, range_map, turn, own, fine, coarse, sections):
    rows, bins = polar.shape
    cols = range_map.shape[2]
    nodes = 2**sections
    chunk = coarse.shape[4] * LANES
    whole = lambda array: pl.BlockSpec(array.shape, lambda i: (0,) * array.ndim)
    return pl.pallas_call(
        functools.partial(tree_kernel, sections),
        grid=(bins // chunk,),
        in_specs=[
            pl.BlockSpec((rows, chunk), lambda i: (0, i)),
            pl.BlockSpec((2, chunk, cols), lambda i: (0, i, 0)),
            whole(turn),
            whole(own),
            whole(fine),
            pl.BlockSpec((1,) + coarse.shape[1:], lambda i: (i, 0, 0, 0, 0)),
        ],
        out_specs=pl.BlockSpec((nodes, rows, cols), lambda i: (0, 0, 0)),
        out_shape=jax.ShapeDtypeStruct((nodes, rows, cols), BF16),
        scratch_shapes=[
            pltpu.VMEM((nodes, rows, chunk), BF16),
            pltpu.VMEM((nodes, rows, 2 * cols), F32),
        ],
        compiler_params=pltpu.CompilerParams(vmem_limit_bytes=52 * 1024 * 1024),
        cost_estimate=pl.CostEstimate(
            flops=40 * 10**9, bytes_accessed=12 * 10**6, transcendentals=0
        ),
        name="tree",
    )(polar, range_map, turn, own, fine, coarse)


def tiles_kernel(slots, place_ref, cover_ref, basis_ref, maps_ref, out_ref):
    e, block = pl.program_id(0), pl.program_id(1)

    @pl.when((e == 0) & (block == 0))
    def _():
        out_ref[...] = jnp.zeros_like(out_ref)

    count, _, rows, beams = maps_ref.shape[1:]
    real = maps_ref[0, :, 0].reshape(count * rows, beams)
    imag = maps_ref[0, :, 1].reshape(count * rows, beams)
    basis = basis_ref[0]
    part_real = mm(jnp.concatenate([real, -imag], axis=1), basis)
    part_imag = mm(jnp.concatenate([imag, real], axis=1), basis)
    first = (place_ref[0] ^ e) * slots + block * count
    for k in range(count):
        tile = cover_ref[first + k]
        out_ref[tile, 0] += part_real[k * rows : (k + 1) * rows]
        out_ref[tile, 1] += part_imag[k * rows : (k + 1) * rows]


def tiles(place, cover, basis, maps, tile_count):
    nodes, slots, _, rows, beams = maps.shape
    block = math.gcd(slots, SLOT_BLOCK)
    cols = basis.shape[2]
    shape = (tile_count, 2, rows, cols)
    return pl.pallas_call(
        functools.partial(tiles_kernel, slots),
        grid_spec=pltpu.PrefetchScalarGridSpec(
            num_scalar_prefetch=2,
            grid=(nodes, slots // block),
            in_specs=[
                pl.BlockSpec((1,) + basis.shape[1:], lambda e, k, p, c: (e, 0, 0)),
                pl.BlockSpec(
                    (1, block, 2, rows, beams), lambda e, k, p, c: (p[0] ^ e, k, 0, 0, 0)
                ),
            ],
            out_specs=pl.BlockSpec(shape, lambda e, k, p, c: (0, 0, 0, 0)),
        ),
        out_shape=jax.ShapeDtypeStruct(shape, F32),
        compiler_params=pltpu.CompilerParams(vmem_limit_bytes=40 * 1024 * 1024),
        cost_estimate=pl.CostEstimate(
            flops=5 * 10**9, bytes_accessed=9 * 10**6, transcendentals=0
        ),
        name="tiles",
    )(place, cover, basis, maps)


def shards(
    raw_echoes,
    chirp_replica,
    steering,
    band_start,
    band_coef,
    phase_rate,
    range_map,
    slot_maps,
    coverage,
):
    pulses, _, range_len = raw_echoes.shape
    tap_count = chirp_replica.shape[1]
    quarter = tap_count // 4
    sections, _, _, _, band, beams = band_coef.shape
    nodes = 2**sections
    subs = lax.axis_size("sub")
    owners = subs * lax.axis_size("rng")
    slot_count = slot_maps.shape[0]
    bins = range_len // 2
    groups = None
    if subs != nodes:
        groups = [list(range(g, g + nodes)) for g in range(0, subs, nodes)]
    place = lax.axis_index("sub") % nodes

    everywhere = (sections, 2, 1, beams)
    cover_row = jnp.pad(coverage[:, 0].astype(F32), (0, beams - slot_count))
    packed = jnp.concatenate(
        [
            band_coef[:, 0].astype(F32).reshape(sections, 2, 2 * band, beams),
            band_start[:, 0].astype(F32)[:, :, None],
            jnp.broadcast_to(phase_rate[:, 0][:, None, None], everywhere),
            jnp.broadcast_to(cover_row, everywhere),
        ],
        axis=2,
    )
    gathered = lax.all_gather(packed, "sub", axis_index_groups=groups)
    maps = lax.all_gather(slot_maps, "sub", axis_index_groups=groups)
    cover = gathered[:, 0, 0, 2 * band + 2, :slot_count].reshape(-1).astype(jnp.int32)
    turn, own = matrices(gathered, place, sections, band)
    rates = gathered[:, :, 1, 2 * band + 1]
    ids = jnp.arange(nodes)
    rate = jnp.stack(
        [
            jnp.sum(jnp.where((ids == place ^ e)[:, None], rates[:, top_bit(e)], 0.0), axis=0)
            for e in range(1, nodes)
        ]
    )
    unit = 2.0 * math.pi / bins
    lane = lax.iota(jnp.int32, LANES).astype(F32)
    chunk = 512
    first = (
        lax.axis_index("rng") * bins + lax.iota(jnp.int32, bins // LANES) * LANES
    ).astype(F32)
    fine_angle = rate[:, :, None] * lane * unit
    fine = jnp.stack([jnp.cos(fine_angle), jnp.sin(fine_angle)], axis=1)
    coarse_angle = rate[:, :, None] * first * unit
    coarse = jnp.stack([jnp.cos(coarse_angle), jnp.sin(coarse_angle)], axis=1)
    coarse = coarse.reshape(nodes - 1, 2, beams, bins // chunk, chunk // LANES)
    coarse = jnp.transpose(coarse, (3, 0, 1, 2, 4))

    raw = raw_echoes.reshape(2 * pulses, range_len)
    halo = from_behind(raw_echoes[:, :, :tap_count], "rng", -1).reshape(2 * pulses, tap_count)
    taps = toeplitz_taps(chirp_replica, quarter, 6 * quarter)
    taps = taps.reshape(6 * quarter, 2 * quarter)
    real, imag = steering[0, 0], steering[0, 1]
    steer = jnp.concatenate(
        [
            jnp.stack([real, -imag], axis=2).reshape(beams, 2 * pulses),
            jnp.stack([imag, real], axis=2).reshape(beams, 2 * pulses),
        ],
        axis=0,
    )
    polar = front(steer, taps, raw, halo)
    basis = tree(polar, range_map, turn, own, fine, coarse, sections)
    partial = tiles(place.reshape(1), cover, basis, maps, owners)
    return lax.psum_scatter(partial, ("sub", "rng"), scatter_dimension=0, tiled=True)


def solution(mesh):
    in_specs = (
        P("sub", None, "rng"),
        P(),
        P("sub", None, None, None),
        P(None, "sub", None, None),
        P(None, "sub", None, None, None, None),
        P(None, "sub", None),
        P(None, "rng", None),
        P(("sub", "rng"), None, None, None),
        P(("sub", "rng"), None),
    )
    out_specs = P(("sub", "rng"), None, None, None)
    return jax.shard_map(shards, mesh=mesh, in_specs=in_specs, out_specs=out_specs, check_vma=False)
```

time: 475 us -> 301 us (0.63)
  blocking collectives: 98.7 us -> 0 us
  Pallas kernels: 0 us -> 70.2 us
  other arithmetic: 66.4 us -> 10.3 us
  waiting for transfers between devices: 220 us -> 174 us
  matrix products: 27.9 us -> 0 us
  local copies, waits for them, and re-layouts: 51.2 us -> 31.3 us
  between operations: 0.42 us -> 13.4 us
  starting transfers between devices: 9.89 us -> 1.38 us
    ppermute x4 -> x0, waiting for transfers between devices: 219 us -> none  [swapped(): return lax.ppermute(value, axis, pairs)]
    reduce_scatter x0 -> x1, waiting for transfers between devices: none -> 136 us  [shards(): lax.psum_scatter(partial, ('sub', 'rng'), scatter_dimension=0, tiled=True)]
    all_to_all x1 -> x0, blocking collectives: 98.7 us -> none  [shards(): lax.all_to_all(outgoing, ('sub', 'rng'), split_axis=0, concat_axis=0, til...]
    pallas_call x0 -> x4, Pallas kernels: none -> 70.2 us  [the longest x1 51.8 us: tree(): pl.pallas_call(functools.partial(tree_kernel, sections), grid=(bins // ch...]
    another operation x10 -> x17, other arithmetic: 43.3 us -> 2.59 us  [the longest x1 1.47 us: shards(): fine = jnp.stack([jnp.cos(fine_angle), jnp.sin(fine_angle)], axis=1)]
    all_gather x0 -> x2, waiting for transfers between devices: none -> 38 us  [the longest x1 33.4 us: shards(): gathered = lax.all_gather(packed, 'sub', axis_index_groups=groups)]
    dot_general x13 -> x0, matrix products: 27.9 us -> none  [the longest x8 14.1 us: complex_apply(): jnp.einsum('cbe,der->cdbr', matrix, field, preferred_element_type=jnp.flo...]
    unnamed x23 -> x12, local copies, waits for them, and re-layouts: 30.9 us -> 8.67 us
  transfers between devices with their start and end apart: 5 -> 4, of which waited for: 5 -> 3; matrix products, arithmetic and copies ran while one was open for 2% -> 10% of each run, Pallas kernels for 0% -> 21%
where the time goes in v1:
time: 301 us; the launch traced here: 300 us
  waiting for transfers between devices  174 us (58%)
  Pallas kernels  70.2 us (23%)
  local copies, waits for them, and re-layouts  31.3 us (10%)
  between operations  13.4 us (4%)
  other arithmetic  10.3 us (3%)
    reduce_scatter x1, waiting for transfers between devices, shards(): lax.psum_scatter(partial, ('sub', 'rng'), scatter_dimension=0, tiled=True)  136 us
    pallas_call x1, Pallas kernels, tree(): pl.pallas_call(functools.partial(tree_kernel, sections), grid=(bins // ch...  51.8 us
    all_gather x1, waiting for transfers between devices, shards(): gathered = lax.all_gather(packed, 'sub', axis_index_groups=groups)  33.4 us
    unnamed x12, local copies, waits for them, and re-layouts  8.67 us
    another operation x1, local copies, waits for them, and re-layouts, shards(): coarse = jnp.stack([jnp.cos(coarse_angle), jnp.sin(coarse_angle)], axis=1)  7.75 us
    reshape x1, local copies, waits for them, and re-layouts, shards(): raw = raw_echoes.reshape(2 * pulses, range_len)  7.23 us
    pallas_call x1, Pallas kernels, tiles(): pl.pallas_call(functools.partial(tiles_kernel, slots), grid_spec=pltpu.Pr...  7.16 us
    pallas_call x1, Pallas kernels, front(): pl.pallas_call(front_kernel, grid=(steps,), in_specs=[pl.BlockSpec(steer....  7.05 us
  transfers between devices with their start and end apart: 4, of which 3 were waited for; matrix products, arithmetic and copies ran while one was open for 10% of the time, Pallas kernels for 21%

profile of v1, /device:TPU:0, one launch (start us, length us, event | category | flops | bytes accessed | tf_op | source)
XLA Modules:
  0.0 300.2 jit_solution(8977853039874943502)
XLA Ops:
  6.5 0.7 convert_bitcast_fusion
  7.2 0.7 fusion.5
  7.9 0.8 copy.68
  8.7 0.7 broadcast_in_dim.128
  9.4 0.7 pad_maximum_fusion.3
  10.0 0.0 all-gather.5.cloned.1.call-update
  10.1 0.0 all-gather.7.cloned.1.call-start
  10.1 1.1 slice.45
  11.3 1.3 collective-permute-start
  12.6 0.0 all-gather.7.cloned.1.call-update
  12.6 0.0 reduce-scatter.2.cloned.1.call-start
  12.6 0.1 fusion.6
  12.7 0.1 fusion.24
  12.8 0.1 fusion.20
  12.9 0.1 fusion.22
  13.0 0.1 fusion.25
  13.0 0.1 fusion.27
  13.1 0.1 fusion.7
  13.2 0.1 fusion.29
  13.3 0.1 fusion.9
  13.3 0.1 fusion.31
  13.5 0.1 fusion.11
  13.6 0.1 fusion.13
  13.6 0.1 fusion.15
  13.7 0.1 fusion.17
  13.8 0.8 fusion.33
  14.6 0.8 slice_bitcast_fusion
  15.4 0.0 copy-start.5
  15.4 7.2 %reshape.161.raw_ref.next_ref = bf16[256,8192]{1,0:T(8,128)(2,1)} reshape(bf16[128,2,8192]{2,1,0:T(2,128)(2,1)} %param.9) | data formatting | bytes 8388608 | tf_op jit(solution)/shard_map/reshape | solution.py:342
  22.6 0.1 copy.72
  22.8 0.1 copy.74
  22.9 0.1 copy.71
  23.0 0.1 copy.73
  23.2 1.1 tile.10
  24.3 0.3 slice.52
  24.6 0.2 reshape.160
  24.8 0.2 copy.75
  25.0 0.1 stack.385
  25.1 0.1 reshape.163.pick_ref
  25.2 0.1 reshape.162.halo_ref
  25.4 2.2 copy-done
  27.6 7.0 %front.1.polar_ref = bf16[256,4096]{1,0:T(8,128)(2,1)S(1)} custom-call(bf16[256,256]{1,0:T(8,128)(2,1)S(1)} %pad_maximum_fusion.2.steer_ref, bf16[768,256]{1,0:T(8,128)(2,1)S(1)} %bitcast.127, bf16[256,8192]{1,0:T(8,128)(2,1)S(1)} %copy-done, bf16[256,8192]{1,0:T(8,128)(2,1)S(1)} %copy-done, bf16[256,512]{1,0:T(8,128)(2,1)S(1)} %reshape.162.halo_ref), custom_call_target="tpu_custom_call" | custom-call | flops 8000000000 | bytes 7000000 | tf_op jit(solution)/shard_map/front/pallas_call | solution.py:59
  34.6 1.4 copy-done.4
  36.0 33.4 %all-gather.5.cloned.1.call-done = f32[64,2,19,128]{3,1,2,0:T(2,128)} async-done(((f32[4,2,19,128]{3,1,2,0:T(2,128)}), f32[64,2,19,128]{3,1,2,0:T(2,128)}) %all-gather.5.cloned.1.call-update) | async-done | bytes 1245200 | tf_op jit(solution)/shard_map/all_gather | solution.py:317
  69.4 1.4 copy.70
  70.9 0.1 convert_element_type.54.cover_ref
  71.0 0.1 select_reduce_fusion.14
  71.1 0.1 select_reduce_fusion.12
  71.2 0.1 select_reduce_fusion.8
  71.3 0.1 select_reduce_fusion
  71.4 0.1 stack.401
  71.5 0.9 fusion.3
  72.4 7.8 %copy.79 = f32[15,2,128,8,4]{4,2,1,0,3:T(8,128)} copy(f32[15,2,128,8,4]{2,3,4,1,0:T(8,128)S(1)} %pad_maximum_fusion.1) | data formatting | bytes 983040 | tf_op jit(solution)/shard_map/stack | solution.py:338
  80.2 3.5 %fusion.1 = (f32[15,1,128,128]{3,2,1,0:T(8,128)S(1)}, f32[15,1,128,128]{3,2,1,0:T(8,128)S(1)}) fusion(f32[128]{0:T(128)S(1)} %iota_convert_fusion, f32[15,128]{1,0:T(8,128)S(1)} %stack.401), kind=kLoop, calls=%fused_computation.3 | loop fusion | flops 491520 | bytes 1974272 | tf_op jit(solution)/shard_map/cos | solution.py:336
  83.7 1.5 pad_maximum_fusion.fine_ref
  85.2 4.2 %matrices.1 = (bf16[15,256,256]{2,1,0:T(8,128)(2,1)S(1)}, bf16[8,256,256]{2,1,0:T(8,128)(2,1)S(1)}) custom-call(s32[90]{0:T(128)S(1)} %reshape.163.pick_ref, f32[16,4,2,19,128]{4,3,2,1,0:T(8,128)S(1)} %bitcast.126), custom_call_target="tpu_custom_call" | custom-call | flops 5000000000 | bytes 5000000 | tf_op jit(solution)/shard_map/matrices/pallas_call | solution.py:134
  89.4 1.3 copy-done.3
  90.7 51.8 %tree.1.basis_ref = bf16[16,256,256]{2,1,0:T(8,128)(2,1)} custom-call(bf16[256,4096]{1,0:T(8,128)(2,1)} %copy-done.4, bf16[2,4096,256]{2,1,0:T(8,128)(2,1)} %map_ref.1, bf16[15,256,256]{2,1,0:T(8,128)(2,1)} %copy-done.3, bf16[8,256,256]{2,1,0:T(8,128)(2,1)S(1)} %get-tuple-element.8.own_ref, f32[15,2,128,128]{3,2,1,0:T(8,128)} %pad_maximum_fusion.fine_ref, ...), custom_call_target="tpu_custom_call" | custom-call | flops 40000000000 | bytes 12000000 | tf_op jit(solution)/shard_map/tree/pallas_call | solution.py:209
  142.5 4.6 %all-gather.7.cloned.1.call-done = bf16[256,2,32,128]{3,2,1,0:T(8,128)(2,1)} async-done(((bf16[16,2,32,128]{3,2,1,0:T(8,128)(2,1)}), bf16[256,2,32,128]{3,2,1,0:T(8,128)(2,1)}) %all-gather.7.cloned.1.call-update) | async-done | bytes 4194320 | tf_op jit(solution)/shard_map/all_gather | solution.py:318
  147.2 2.2 copy-done.1
  149.4 1.6 copy-done.2
  150.9 7.2 %tiles.1 = f32[32,2,32,256]{3,2,1,0:T(8,128)} custom-call(s32[1]{0:T(128)} %bitcast.place_ref, s32[256]{0:T(256)S(1)} %convert_element_type.54.cover_ref, bf16[16,256,256]{2,1,0:T(8,128)(2,1)S(1)} %copy-done.2, bf16[16,16,2,32,128]{4,3,2,1,0:T(8,128)(2,1)S(1)} %bitcast.128), custom_call_target="tpu_custom_call" | custom-call | flops 5000000000 | bytes 9000000 | tf_op jit(solution)/shard_map/tiles/pallas_call | solution.py:259
  158.1 0.0 reduce-scatter.2.cloned.1.call-update
  158.1 135.5 %reduce-scatter.2.cloned.1.call-done = f32[1,2,32,256]{3,2,1,0:T(8,128)} async-done(((f32[32,2,32,256]{3,2,1,0:T(8,128)}), f32[1,2,32,256]{3,2,1,0:T(8,128)}) %reduce-scatter.2.cloned.1.call-update) | async-done | bytes 65552 | tf_op jit(solution)/shard_map/reduce_scatter | solution.py:357
  (29 shorter events, 0.3 us)
Async XLA Ops:
  6.5 62.9 %all-gather.5.cloned.1.call-start = ((), (), s32[]{:S(2)}) async-start(), calls=%async_computation.2 | async-start | bytes 1323008 | tf_op jit(solution)/shard_map/all_gather | solution.py:317
  10.1 137.1 %all-gather.7.cloned.1.call-start = ((), (), s32[]{:S(2)}) async-start(), calls=%async_computation.3 | async-start | bytes 4456448 | tf_op jit(solution)/shard_map/all_gather | solution.py:318
  11.3 14.0 %collective-permute-start = (bf16[128,2,512]{2,1,0:T(2,128)(2,1)S(1)}, bf16[128,2,512]{2,1,0:T(2,128)(2,1)S(1)}, u32[]{:S(2)}, u32[]{:S(2)}) collective-permute-start(bf16[128,2,512]{2,1,0:T(2,128)(2,1)S(1)} %slice.45), channel_id=1, source_target_pairs={{1,0},{3,2},{5,4},{7,6},{9,8},{11,10},{13,12},{15,14},{17,16},{19,... | collective-permute-start | bytes 786440 | tf_op jit(solution)/shard_map/ppermute | solution.py:24
  12.6 281.1 %reduce-scatter.2.cloned.1.call-start = ((), (), s32[]{:S(2)}) async-start(), calls=%async_computation.1 | async-start | bytes 2162688 | tf_op jit(solution)/shard_map/reduce_scatter | solution.py:357
  15.4 7.7 %copy-start.5 = (bf16[2,512]{1,0:T(2,128)(2,1)S(1)}, bf16[2,512]{1,0:T(2,128)(2,1)}, u32[]{:S(2)}) copy-start(bf16[2,512]{1,0:T(2,128)(2,1)} %param.10) | copy-start | bytes 6148
  25.4 2.2 copy-start
  34.6 1.4 copy-start.4
  89.3 1.3 copy-start.3
  147.2 2.2 copy-start.1
  149.4 1.6 copy-start.2
Sparse Core Ops, SparseCore 0:
  10.2 59.1 all-gather.4
  72.2 74.9 all-gather.6
  158.2 135.3 reduce-scatter.1

commit v2 on v1

--- a/solution.py
+++ b/solution.py
@@ -22,6 +22,12 @@
     count = lax.axis_size(axis)
     initial, last = (max(0, -steps), min(count, count - steps))
     return lax.ppermute(value, axis, [(source, source + steps) for source in range(initial, last)])
+
+
+def swapped(value, axis, distance):
+    mask = 2**distance
+    pairs = [(source, source ^ mask) for source in range(lax.axis_size(axis))]
+    return lax.ppermute(value, axis, pairs)
 
 
 def toeplitz_taps(replica, quarter, window_width):
@@ -125,12 +131,12 @@
             own_ref[e] = chain.astype(F32).T.astype(BF16)
 
 
-def matrices(data, place, sections, taps):
+def matrices(data, spot, sections, taps):
     nodes = 2**sections
     beams = data.shape[4]
     wanted = [(e, top_bit(e), 1) for e in range(1, nodes)]
     wanted += [(e, s, 0) for s, e in own_list(sections)]
-    picks = jnp.stack([jnp.stack([place ^ e, place * 0 + s, place * 0 + j]) for e, s, j in wanted])
+    picks = jnp.array([[spot[e], s, j] for e, s, j in wanted], jnp.int32)
     return pl.pallas_call(
         functools.partial(matrices_kernel, sections, taps),
         grid_spec=pltpu.PrefetchScalarGridSpec(
@@ -244,7 +250,7 @@
     basis = basis_ref[0]
     part_real = mm(jnp.concatenate([real, -imag], axis=1), basis)
     part_imag = mm(jnp.concatenate([imag, real], axis=1), basis)
-    first = (place_ref[0] ^ e) * slots + block * count
+    first = e * slots + block * count
     for k in range(count):
         tile = cover_ref[first + k]
         out_ref[tile, 0] += part_real[k * rows : (k + 1) * rows]
@@ -314,17 +320,16 @@
         ],
         axis=2,
     )
-    gathered = lax.all_gather(packed, "sub", axis_index_groups=groups)
+    relative = packed[None]
+    for bit in reversed(range(sections)):
+        relative = jnp.concatenate([relative, swapped(relative, "sub", bit)], axis=0)
+    spot = [sum(((e >> b) & 1) << (sections - 1 - b) for b in range(sections)) for e in range(nodes)]
     maps = lax.all_gather(slot_maps, "sub", axis_index_groups=groups)
-    cover = gathered[:, 0, 0, 2 * band + 2, :slot_count].reshape(-1).astype(jnp.int32)
-    turn, own = matrices(gathered, place, sections, band)
-    rates = gathered[:, :, 1, 2 * band + 1]
-    ids = jnp.arange(nodes)
+    cover = jnp.concatenate([relative[n, 0, 0, 2 * band + 2, :slot_count] for n in spot])
+    cover = cover.astype(jnp.int32)
+    turn, own = matrices(relative, spot, sections, band)
     rate = jnp.stack(
-        [
-            jnp.sum(jnp.where((ids == place ^ e)[:, None], rates[:, top_bit(e)], 0.0), axis=0)
-            for e in range(1, nodes)
-        ]
+        [relative[spot[e], top_bit(e), 1, 2 * band + 1] for e in range(1, nodes)]
     )
     unit = 2.0 * math.pi / bins
     lane = lax.iota(jnp.int32, LANES).astype(F32)
@@ -354,7 +359,16 @@
     polar = front(steer, taps, raw, halo)
     basis = tree(polar, range_map, turn, own, fine, coarse, sections)
     partial = tiles(place.reshape(1), cover, basis, maps, owners)
-    return lax.psum_scatter(partial, ("sub", "rng"), scatter_dimension=0, tiled=True)
+    cores = lax.axis_size("rng")
+    partial = partial.reshape((subs, cores) + partial.shape[1:])
+    core = lax.axis_index("rng")
+    half = lax.dynamic_index_in_dim(partial, core, 1, keepdims=False)
+    for step in range(1, cores):
+        away = lax.dynamic_index_in_dim(partial, (core + step) % cores, 1, keepdims=False)
+        pairs = [(c, (c + step) % cores) for c in range(cores)]
+        half = half + lax.ppermute(away.astype(BF16), "rng", pairs).astype(F32)
+    received = lax.all_to_all(half.astype(BF16), "sub", split_axis=0, concat_axis=0, tiled=True)
+    return jnp.sum(received.astype(F32), axis=0, keepdims=True)
 
 
 def solution(mesh):

time: 301 us -> 189 us (0.63)
  waiting for transfers between devices: 174 us -> 29.5 us
  blocking collectives: 0 us -> 19.1 us
  starting transfers between devices: 1.38 us -> 10.4 us
  local copies, waits for them, and re-layouts: 31.3 us -> 36 us
    reduce_scatter x1 -> x0, waiting for transfers between devices: 136 us -> none  [shards(): lax.psum_scatter(partial, ('sub', 'rng'), scatter_dimension=0, tiled=True)]
    all_gather x1 -> x0, waiting for transfers between devices: 33.4 us -> none  [shards(): gathered = lax.all_gather(packed, 'sub', axis_index_groups=groups)]
    ppermute x0 -> x5, waiting for transfers between devices: none -> 29.4 us  [the longest x4 27.6 us: swapped(): return lax.ppermute(value, axis, pairs)]
    all_to_all x0 -> x1, blocking collectives: none -> 19.1 us  [shards(): lax.all_to_all(half.astype(BF16), 'sub', split_axis=0, concat_axis=0, til...]
    ppermute x0 -> x5, starting transfers between devices: none -> 9.13 us  [the longest x4 9.05 us: swapped(): return lax.ppermute(value, axis, pairs)]
    all_gather x1, waiting for transfers between devices: 4.63 us -> 0.01 us  [shards(): maps = lax.all_gather(slot_maps, 'sub', axis_index_groups=groups)]
    unnamed x12 -> x27, local copies, waits for them, and re-layouts: 8.67 us -> 8.68 us
  transfers between devices with their start and end apart: 4 -> 7, of which waited for: 3 -> 4; matrix products, arithmetic and copies ran while one was open for 10% -> 18% of each run, Pallas kernels for 21% -> 33%
where the time goes in v2:
time: 189 us; the launch traced here: 188 us
  Pallas kernels  68.8 us (36%)
  local copies, waits for them, and re-layouts  36 us (19%)
  waiting for transfers between devices  29.5 us (16%)
  blocking collectives  19.1 us (10%)
  between operations  13.8 us (7%)
  other arithmetic  10.6 us (6%)
  starting transfers between devices  10.4 us (6%)
    pallas_call x1, Pallas kernels, tree(): pl.pallas_call(functools.partial(tree_kernel, sections), grid=(bins // ch...  51.8 us
    ppermute x4, waiting for transfers between devices, swapped(): return lax.ppermute(value, axis, pairs)  27.6 us
    all_to_all x1, blocking collectives, shards(): lax.all_to_all(half.astype(BF16), 'sub', split_axis=0, concat_axis=0, til...  19.1 us
    ppermute x4, starting transfers between devices, swapped(): return lax.ppermute(value, axis, pairs)  9.05 us
    unnamed x27, local copies, waits for them, and re-layouts  8.68 us
    another operation x1, local copies, waits for them, and re-layouts, shards(): coarse = jnp.stack([jnp.cos(coarse_angle), jnp.sin(coarse_angle)], axis=1)  7.68 us
    reshape x1, local copies, waits for them, and re-layouts, shards(): raw = raw_echoes.reshape(2 * pulses, range_len)  7.19 us
    pallas_call x1, Pallas kernels, front(): pl.pallas_call(front_kernel, grid=(steps,), in_specs=[pl.BlockSpec(steer....  6.99 us
  transfers between devices with their start and end apart: 7, of which 4 were waited for; matrix products, arithmetic and copies ran while one was open for 18% of the time, Pallas kernels for 33%

profile of v2, /device:TPU:0, one launch (start us, length us, event | category | flops | bytes accessed | tf_op | source)
XLA Modules:
  0.0 188.2 jit_solution(1088995927395381023)
XLA Ops:
  6.5 0.0 all-gather.3.cloned.1.call-start
  6.5 0.7 convert_bitcast_fusion
  7.2 0.7 bitcast_convert_fusion.1
  7.9 0.8 bitcast_convert_fusion
  8.7 0.7 broadcast_in_dim.11
  9.4 4.1 %collective-permute-start = (f32[1,4,2,19,128]{4,3,2,1,0:T(8,128)S(1)}, f32[1,4,2,19,128]{4,3,2,1,0:T(8,128)S(1)}, u32[]{:S(2)}, u32[]{:S(2)}) collective-permute-start(f32[1,4,2,19,128]{4,3,2,1,0:T(8,128)S(1)} %maximum_bitcast_fusion), channel_id=1, source_target_pairs={{0,16},{2,18},{4,20},{6,22},{8,24},{10,26},{12,28},{14,30},{16,0},... | collective-permute-start | bytes 233480 | tf_op jit(solution)/shard_map/ppermute | solution.py:30
  13.5 1.8 slice.124
  15.3 1.3 collective-permute-start.4
  16.6 0.0 all-gather.3.cloned.1.call-update
  16.6 0.6 slice_bitcast_fusion.32
  17.2 0.8 fusion.6
  18.0 0.8 slice_bitcast_fusion
  18.7 7.2 %reshape.104.raw_ref.next_ref = bf16[256,8192]{1,0:T(8,128)(2,1)} reshape(bf16[128,2,8192]{2,1,0:T(2,128)(2,1)} %param.10) | data formatting | bytes 8388608 | tf_op jit(solution)/shard_map/reshape | solution.py:347
  26.0 0.1 copy.23
  26.1 0.1 copy.25
  26.2 0.1 copy.22
  26.4 0.1 copy.24
  26.5 0.0 copy-done.6
  26.6 1.1 tile.10
  27.7 0.3 slice.156
  27.9 0.2 reshape.103
  28.2 0.2 copy.26
  28.4 0.6 iota_convert_fusion
  29.0 0.0 collective-permute-done
  29.0 1.6 collective-permute-start.1
  30.7 0.5 slice_bitcast_fusion.24
  31.2 0.5 slice_bitcast_fusion.9
  31.8 7.8 %collective-permute-done.1 = f32[2,4,2,19,128]{4,3,2,1,0:T(8,128)S(1)} collective-permute-done((f32[2,4,2,19,128]{4,3,2,1,0:T(8,128)S(1)}, f32[2,4,2,19,128]{4,3,2,1,0:T(8,128)S(1)}, u32[]{:S(2)}, u32[]{:S(2)}) %collective-permute-start.1) | collective-permute-done | bytes 155680 | tf_op jit(solution)/shard_map/ppermute | solution.py:30
  39.6 1.6 collective-permute-start.2
  41.2 0.6 slice_bitcast_fusion.20
  41.8 0.0 collective-permute-done.4
  41.8 1.1 reshape.105.halo_ref
  42.9 12.3 %collective-permute-done.2 = f32[4,4,2,19,128]{4,3,2,1,0:T(8,128)S(1)} collective-permute-done((f32[4,4,2,19,128]{4,3,2,1,0:T(8,128)S(1)}, f32[4,4,2,19,128]{4,3,2,1,0:T(8,128)S(1)}, u32[]{:S(2)}, u32[]{:S(2)}) %collective-permute-start.2) | collective-permute-done | bytes 311328 | tf_op jit(solution)/shard_map/ppermute | solution.py:30
  55.2 0.1 pad_maximum_fusion.1
  55.3 0.4 copy.21
  55.7 1.7 collective-permute-start.3
  57.4 2.2 %copy-done = bf16[256,8192]{1,0:T(8,128)(2,1)S(1)} copy-done((bf16[256,8192]{1,0:T(8,128)(2,1)S(1)}, bf16[256,8192]{1,0:T(8,128)(2,1)}, u32[]{:S(2)}) %copy-start) | copy-done | bytes 4194328
  59.6 7.0 %front.1.polar_ref = bf16[256,4096]{1,0:T(8,128)(2,1)S(1)} custom-call(bf16[256,256]{1,0:T(8,128)(2,1)S(1)} %pad_maximum_fusion.5.steer_ref, bf16[768,256]{1,0:T(8,128)(2,1)S(1)} %bitcast.97, bf16[256,8192]{1,0:T(8,128)(2,1)S(1)} %copy-done, bf16[256,8192]{1,0:T(8,128)(2,1)S(1)} %copy-done, bf16[256,512]{1,0:T(8,128)(2,1)S(1)} %reshape.105.halo_ref), custom_call_target="tpu_custom_call" | custom-call | flops 8000000000 | bytes 7000000 | tf_op jit(solution)/shard_map/front/pallas_call | solution.py:65
  66.6 1.4 copy-done.5
  68.0 7.4 %collective-permute-done.3 = f32[8,4,2,19,128]{4,0,3,2,1:T(8,128)} collective-permute-done((f32[8,4,2,19,128]{4,0,3,2,1:T(8,128)S(1)}, f32[8,4,2,19,128]{4,0,3,2,1:T(8,128)}, u32[]{:S(2)}, u32[]{:S(2)}) %collective-permute-start.3) | collective-permute-done | bytes 622624 | tf_op jit(solution)/shard_map/ppermute | solution.py:30
  75.4 1.0 slice_bitcast_fusion.17
  76.4 0.1 concatenate.32
  76.5 0.8 slice_bitcast_fusion.2
  77.3 0.0 copy-done.10
  77.4 0.1 stack.22
  77.4 0.9 fusion.5
  78.4 0.0 copy-start.8
  78.4 7.7 %copy.28 = f32[15,2,128,8,4]{4,2,1,0,3:T(8,128)} copy(f32[15,2,128,8,4]{2,3,4,1,0:T(8,128)S(1)} %pad_maximum_fusion.2) | data formatting | bytes 983040 | tf_op jit(solution)/shard_map/stack | solution.py:343
  86.1 3.5 %fusion.2 = (f32[15,1,128,128]{3,2,1,0:T(8,128)S(1)}, f32[15,1,128,128]{3,2,1,0:T(8,128)S(1)}) fusion(f32[128]{0:T(128)S(1)} %copy-done.8, f32[15,128]{1,0:T(8,128)S(1)} %stack.22), kind=kLoop, calls=%fused_computation.7 | loop fusion | flops 491520 | bytes 1974272 | tf_op jit(solution)/shard_map/cos | solution.py:341
  89.6 0.0 copy-start.2
  89.6 1.6 pad_maximum_fusion.fine_ref
  91.2 1.2 copy_dynamic-update-slice_fusion.data_ref
  92.4 4.2 %matrices.1 = (bf16[15,256,256]{2,1,0:T(8,128)(2,1)S(1)}, bf16[8,256,256]{2,1,0:T(8,128)(2,1)S(1)}) custom-call(s32[90]{0:T(128)S(1)} %copy-done.2, f32[16,4,2,19,128]{4,3,2,1,0:T(8,128)S(1)} %copy_dynamic-update-slice_fusion.data_ref), custom_call_target="tpu_custom_call" | custom-call | flops 5000000000 | bytes 5000000 | tf_op jit(solution)/shard_map/matrices/pallas_call | solution.py:140
  96.6 1.3 copy-done.4
  97.8 51.8 %tree.1.basis_ref = bf16[16,256,256]{2,1,0:T(8,128)(2,1)} custom-call(bf16[256,4096]{1,0:T(8,128)(2,1)} %copy-done.5, bf16[2,4096,256]{2,1,0:T(8,128)(2,1)} %map_ref.1, bf16[15,256,256]{2,1,0:T(8,128)(2,1)} %copy-done.4, bf16[8,256,256]{2,1,0:T(8,128)(2,1)S(1)} %get-tuple-element.8.own_ref, f32[15,2,128,128]{3,2,1,0:T(8,128)} %pad_maximum_fusion.fine_ref, ...), custom_call_target="tpu_custom_call" | custom-call | flops 40000000000 | bytes 12000000 | tf_op jit(solution)/shard_map/tree/pallas_call | solution.py:215
  149.6 2.2 %copy-done.1 = bf16[256,2,32,128]{3,2,1,0:T(8,128)(2,1)S(1)} copy-done((bf16[256,2,32,128]{3,2,1,0:T(8,128)(2,1)S(1)}, bf16[256,2,32,128]{3,2,1,0:T(8,128)(2,1)}, u32[]{:S(2)}) %copy-start.1) | copy-done | bytes 4194328
  151.8 1.6 copy-done.3
  153.4 5.8 %tiles.1 = f32[32,2,32,256]{3,2,1,0:T(8,128)S(1)} custom-call(s32[1]{0:T(128)} %bitcast.place_ref, s32[256]{0:T(256)S(1)} %convert_element_type.66.cover_ref, bf16[16,256,256]{2,1,0:T(8,128)(2,1)S(1)} %copy-done.3, bf16[16,16,2,32,128]{4,3,2,1,0:T(8,128)(2,1)S(1)} %bitcast.98), custom_call_target="tpu_custom_call" | custom-call | flops 5000000000 | bytes 9000000 | tf_op jit(solution)/shard_map/tiles/pallas_call | solution.py:265
  159.2 0.1 fusion.3
  159.3 0.1 collective-permute-start.5
  159.4 1.9 %collective-permute-done.5 = bf16[16,2,32,256]{3,2,1,0:T(8,128)(2,1)S(1)} collective-permute-done((bf16[16,2,32,256]{3,2,1,0:T(8,128)(2,1)S(1)}, bf16[16,2,32,256]{3,2,1,0:T(8,128)(2,1)S(1)}, u32[]{:S(2)}, u32[]{:S(2)}) %collective-permute-start.5) | collective-permute-done | bytes 524320 | tf_op jit(solution)/shard_map/ppermute | solution.py:369
  161.3 0.2 fusion
  161.5 19.1 %all_to_all.5 = bf16[16,2,32,256]{3,2,1,0:T(8,128)(2,1)S(1)} all-to-all(bf16[16,2,32,256]{3,2,1,0:T(8,128)(2,1)S(1)} %fusion), channel_id=1, replica_groups=mesh['sub'=16,'rng'=2] {'sub'}, dimensions={0} | all-to-all | bytes 1048576 | tf_op jit(solution)/shard_map/all_to_all | solution.py:370
  180.6 0.7 convert_reduce_fusion
  (35 shorter events, 0.3 us)
Async XLA Ops:
  6.5 143.1 %all-gather.3.cloned.1.call-start = ((), (), s32[]{:S(2)}) async-start(), calls=%async_computation.1 | async-start | bytes 4456448 | tf_op jit(solution)/shard_map/all_gather | solution.py:327
  9.4 19.6 %collective-permute-start = (f32[1,4,2,19,128]{4,3,2,1,0:T(8,128)S(1)}, f32[1,4,2,19,128]{4,3,2,1,0:T(8,128)S(1)}, u32[]{:S(2)}, u32[]{:S(2)}) collective-permute-start(f32[1,4,2,19,128]{4,3,2,1,0:T(8,128)S(1)} %maximum_bitcast_fusion), channel_id=1, source_target_pairs={{0,16},{2,18},{4,20},{6,22},{8,24},{10,26},{12,28},{14,30},{16,0},... | collective-permute-start | bytes 233480 | tf_op jit(solution)/shard_map/ppermute | solution.py:30
  15.3 26.5 %collective-permute-start.4 = (bf16[128,2,512]{2,1,0:T(2,128)(2,1)}, bf16[128,2,512]{2,1,0:T(2,128)(2,1)}, u32[]{:S(2)}, u32[]{:S(2)}) collective-permute-start(bf16[128,2,512]{2,1,0:T(2,128)(2,1)} %slice.124), channel_id=1, source_target_pairs={{1,0},{3,2},{5,4},{7,6},{9,8},{11,10},{13,12},{15,14},{17,16},{19,... | collective-permute-start | bytes 786440 | tf_op jit(solution)/shard_map/ppermute | solution.py:24
  18.7 7.7 %copy-start.6 = (bf16[2,512]{1,0:T(2,128)(2,1)S(1)}, bf16[2,512]{1,0:T(2,128)(2,1)}, u32[]{:S(2)}) copy-start(bf16[2,512]{1,0:T(2,128)(2,1)} %param.11) | copy-start | bytes 6148
  29.0 10.5 %collective-permute-start.1 = (f32[2,4,2,19,128]{4,3,2,1,0:T(8,128)S(1)}, f32[2,4,2,19,128]{4,3,2,1,0:T(8,128)S(1)}, u32[]{:S(2)}, u32[]{:S(2)}) collective-permute-start(f32[2,4,2,19,128]{4,3,2,1,0:T(8,128)S(1)} %pad_maximum_fusion.4), channel_id=1, source_target_pairs={{0,8},{2,10},{4,12},{6,14},{8,0},{10,2},{12,4},{14,6},{16,24},{18,... | collective-permute-start | bytes 466952 | tf_op jit(solution)/shard_map/ppermute | solution.py:30
  39.6 15.6 %collective-permute-start.2 = (f32[4,4,2,19,128]{4,3,2,1,0:T(8,128)S(1)}, f32[4,4,2,19,128]{4,3,2,1,0:T(8,128)S(1)}, u32[]{:S(2)}, u32[]{:S(2)}) collective-permute-start(f32[4,4,2,19,128]{4,3,2,1,0:T(8,128)S(1)} %pad_maximum_fusion.3), channel_id=1, source_target_pairs={{0,4},{2,6},{4,0},{6,2},{8,12},{10,14},{12,8},{14,10},{16,20},{18,... | collective-permute-start | bytes 933896 | tf_op jit(solution)/shard_map/ppermute | solution.py:30
  55.7 19.7 %collective-permute-start.3 = (f32[8,4,2,19,128]{4,0,3,2,1:T(8,128)S(1)}, f32[8,4,2,19,128]{4,0,3,2,1:T(8,128)}, u32[]{:S(2)}, u32[]{:S(2)}) collective-permute-start(f32[8,4,2,19,128]{4,0,3,2,1:T(8,128)S(1)} %copy.21), channel_id=1, source_target_pairs={{0,2},{2,0},{4,6},{6,4},{8,10},{10,8},{12,14},{14,12},{16,18},{18,... | collective-permute-start | bytes 1867784 | tf_op jit(solution)/shard_map/ppermute | solution.py:30
  57.4 2.2 %copy-start = (bf16[256,8192]{1,0:T(8,128)(2,1)S(1)}, bf16[256,8192]{1,0:T(8,128)(2,1)}, u32[]{:S(2)}) copy-start(bf16[256,8192]{1,0:T(8,128)(2,1)} %reshape.104.raw_ref.next_ref) | copy-start | bytes 12582916
  59.6 16.8 %copy-start.7 = (f32[16]{0:T(128)S(1)}, f32[16]{0:T(128)}, u32[]{:S(2)}) copy-start(f32[16]{0:T(128)} %get-tuple-element.36) | copy-start | bytes 196
  59.6 16.8 %copy-start.9 = (f32[16]{0:T(128)S(1)}, f32[16]{0:T(128)}, u32[]{:S(2)}) copy-start(f32[16]{0:T(128)} %slice_bitcast_fusion.32) | copy-start | bytes 196
  59.6 16.8 %copy-start.11 = (f32[16]{0:T(128)S(1)}, f32[16]{0:T(128)}, u32[]{:S(2)}) copy-start(f32[16]{0:T(128)} %slice_bitcast_fusion.24) | copy-start | bytes 196
  59.6 17.8 %copy-start.10 = (f32[1,128]{1,0:T(1,128)S(1)}, f32[1,128]{1,0:T(1,128)}, u32[]{:S(2)}) copy-start(f32[1,128]{1,0:T(1,128)} %slice_bitcast_fusion.9) | copy-start | bytes 1540
  66.6 1.4 copy-start.5
  78.4 7.7 %copy-start.8 = (f32[128]{0:T(128)S(1)}, f32[128]{0:T(128)}, u32[]{:S(2)}) copy-start(f32[128]{0:T(128)} %iota_convert_fusion) | copy-start | bytes 1540
  89.6 2.8 %copy-start.2 = (s32[90]{0:T(128)S(1)}, s32[90]{0:T(128)}, u32[]{:S(2)}) copy-start(s32[90]{0:T(128)} %constant.66.pick_ref) | copy-start | bytes 1084
  96.6 1.3 copy-start.4
  149.6 2.2 %copy-start.1 = (bf16[256,2,32,128]{3,2,1,0:T(8,128)(2,1)S(1)}, bf16[256,2,32,128]{3,2,1,0:T(8,128)(2,1)}, u32[]{:S(2)}) copy-start(bf16[256,2,32,128]{3,2,1,0:T(8,128)(2,1)} %all-gather.3.cloned.1.call-done) | copy-start | bytes 12582916
  151.8 1.6 copy-start.3
  159.3 2.0 %collective-permute-start.5 = (bf16[16,2,32,256]{3,2,1,0:T(8,128)(2,1)S(1)}, bf16[16,2,32,256]{3,2,1,0:T(8,128)(2,1)S(1)}, u32[]{:S(2)}, u32[]{:S(2)}) collective-permute-start(bf16[16,2,32,256]{3,2,1,0:T(8,128)(2,1)S(1)} %fusion.3), channel_id=1, source_target_pairs={{0,1},{1,0},{2,3},{3,2},{4,5},{5,4},{6,7},{7,6},{8,9},{9,8},{10,11... | collective-permute-start | bytes 1572872 | tf_op jit(solution)/shard_map/ppermute | solution.py:369
Sparse Core Ops, SparseCore 0:
  16.7 79.4 all-gather.2

commit v3 on v2

--- a/solution.py
+++ b/solution.py
@@ -184,10 +184,13 @@
         parent = e ^ (2 ** top_bit(e))
         merged = mm(turn_ref[e - 1], field[parent])
         fine_cos, fine_sin = fine_ref[e - 1, 0], fine_ref[e - 1, 1]
+        back = lax.rem(LANES - step * (width // LANES), LANES)
+        coarse_cos = pltpu.roll(coarse_ref[e - 1, 0], back, 1)
+        coarse_sin = pltpu.roll(coarse_ref[e - 1, 1], back, 1)
         for j in range(width // LANES):
             at = slice(j * LANES, (j + 1) * LANES)
-            c = coarse_ref[0, e - 1, 0, :, j : j + 1]
-            s = coarse_ref[0, e - 1, 1, :, j : j + 1]
+            c = coarse_cos[:, j : j + 1]
+            s = coarse_sin[:, j : j + 1]
             cosine = fine_cos * c - fine_sin * s
             sine = fine_cos * s + fine_sin * c
             real, imag = merged[:beams, at], merged[beams:, at]
@@ -206,11 +209,10 @@
             out_ref[e] = basis
 
 
-def tree(polar, range_map, turn, own, fine, coarse, sections):
+def tree(polar, range_map, turn, own, fine, coarse, sections, chunk):
     rows, bins = polar.shape
     cols = range_map.shape[2]
     nodes = 2**sections
-    chunk = coarse.shape[4] * LANES
     whole = lambda array: pl.BlockSpec(array.shape, lambda i: (0,) * array.ndim)
     return pl.pallas_call(
         functools.partial(tree_kernel, sections),
@@ -221,7 +223,7 @@
             whole(turn),
             whole(own),
             whole(fine),
-            pl.BlockSpec((1,) + coarse.shape[1:], lambda i: (i, 0, 0, 0, 0)),
+            whole(coarse),
         ],
         out_specs=pl.BlockSpec((nodes, rows, cols), lambda i: (0, 0, 0)),
         out_shape=jax.ShapeDtypeStruct((nodes, rows, cols), BF16),
@@ -335,14 +337,12 @@
     lane = lax.iota(jnp.int32, LANES).astype(F32)
     chunk = 512
     first = (
-        lax.axis_index("rng") * bins + lax.iota(jnp.int32, bins // LANES) * LANES
+        lax.axis_index("rng") * bins + lax.iota(jnp.int32, LANES) * LANES
     ).astype(F32)
     fine_angle = rate[:, :, None] * lane * unit
     fine = jnp.stack([jnp.cos(fine_angle), jnp.sin(fine_angle)], axis=1)
     coarse_angle = rate[:, :, None] * first * unit
     coarse = jnp.stack([jnp.cos(coarse_angle), jnp.sin(coarse_angle)], axis=1)
-    coarse = coarse.reshape(nodes - 1, 2, beams, bins // chunk, chunk // LANES)
-    coarse = jnp.transpose(coarse, (3, 0, 1, 2, 4))
 
     raw = raw_echoes.reshape(2 * pulses, range_len)
     halo = from_behind(raw_echoes[:, :, :tap_count], "rng", -1).reshape(2 * pulses, tap_count)
@@ -357,7 +357,7 @@
         axis=0,
     )
     polar = front(steer, taps, raw, halo)
-    basis = tree(polar, range_map, turn, own, fine, coarse, sections)
+    basis = tree(polar, range_map, turn, own, fine, coarse, sections, chunk)
     partial = tiles(place.reshape(1), cover, basis, maps, owners)
     cores = lax.axis_size("rng")
     partial = partial.reshape((subs, cores) + partial.shape[1:])

time: 189 us -> 189 us (level)
  local copies, waits for them, and re-layouts: 36 us -> 28 us
  Pallas kernels: 68.8 us -> 72.7 us
  other arithmetic: 10.6 us -> 14.4 us
    another operation x1 -> x0, local copies, waits for them, and re-layouts: 7.68 us -> none  [shards(): coarse = jnp.stack([jnp.cos(coarse_angle), jnp.sin(coarse_angle)], axis=1)]
    cos x1, other arithmetic: 0.94 us -> 6.93 us  [shards(): coarse = jnp.stack([jnp.cos(coarse_angle), jnp.sin(coarse_angle)], axis=1)]
    pallas_call x1, Pallas kernels: 51.8 us -> 55.6 us  [tree(): pl.pallas_call(functools.partial(tree_kernel, sections), grid=(bins // ch...]
    cos x1 -> x0, other arithmetic: 3.5 us -> none  [shards(): fine = jnp.stack([jnp.cos(fine_angle), jnp.sin(fine_angle)], axis=1)]
  transfers between devices with their start and end apart: 7 -> 7, of which waited for: 4 -> 4; matrix products, arithmetic and copies ran while one was open for 18% -> 16% of each run, Pallas kernels for 33% -> 36%
where the time goes in v3:
time: 189 us; the launch traced here: 188 us
  Pallas kernels  72.7 us (38%)
  waiting for transfers between devices  29.6 us (16%)
  local copies, waits for them, and re-layouts  28 us (15%)
  blocking collectives  19.2 us (10%)
  other arithmetic  14.4 us (8%)
  between operations  13.8 us (7%)
  starting transfers between devices  10.4 us (6%)
    pallas_call x1, Pallas kernels, tree(): pl.pallas_call(functools.partial(tree_kernel, sections), grid=(bins // ch...  55.6 us
    ppermute x4, waiting for transfers between devices, swapped(): return lax.ppermute(value, axis, pairs)  27.7 us
    all_to_all x1, blocking collectives, shards(): lax.all_to_all(half.astype(BF16), 'sub', split_axis=0, concat_axis=0, til...  19.2 us
    ppermute x4, starting transfers between devices, swapped(): return lax.ppermute(value, axis, pairs)  9.09 us
    unnamed x27, local copies, waits for them, and re-layouts  8.69 us
    reshape x1, local copies, waits for them, and re-layouts, shards(): raw = raw_echoes.reshape(2 * pulses, range_len)  7.26 us
    pallas_call x1, Pallas kernels, front(): pl.pallas_call(front_kernel, grid=(steps,), in_specs=[pl.BlockSpec(steer....  6.99 us
    cos x1, other arithmetic, shards(): coarse = jnp.stack([jnp.cos(coarse_angle), jnp.sin(coarse_angle)], axis=1)  6.93 us
  transfers between devices with their start and end apart: 7, of which 4 were waited for; matrix products, arithmetic and copies ran while one was open for 16% of the time, Pallas kernels for 36%

profile of v3, /device:TPU:0, one launch (start us, length us, event | category | flops | bytes accessed | tf_op | source)
XLA Modules:
  0.0 188.1 jit_solution(15327918065570688179)
XLA Ops:
  6.5 0.0 all-gather.3.cloned.1.call-start
  6.5 0.7 convert_bitcast_fusion
  7.2 0.7 bitcast_convert_fusion.1
  7.9 0.8 bitcast_convert_fusion
  8.7 0.7 broadcast_in_dim.11
  9.4 4.1 %collective-permute-start = (f32[1,4,2,19,128]{4,3,2,1,0:T(8,128)S(1)}, f32[1,4,2,19,128]{4,3,2,1,0:T(8,128)S(1)}, u32[]{:S(2)}, u32[]{:S(2)}) collective-permute-start(f32[1,4,2,19,128]{4,3,2,1,0:T(8,128)S(1)} %maximum_bitcast_fusion), channel_id=1, source_target_pairs={{0,16},{2,18},{4,20},{6,22},{8,24},{10,26},{12,28},{14,30},{16,0},... | collective-permute-start | bytes 233480 | tf_op jit(solution)/shard_map/ppermute | solution.py:30
  13.5 1.9 slice.124
  15.3 1.3 collective-permute-start.4
  16.6 0.0 all-gather.3.cloned.1.call-update
  16.7 0.6 slice_bitcast_fusion.32
  17.2 0.8 fusion.6
  18.0 0.8 slice_bitcast_fusion
  18.8 7.3 %reshape.97.raw_ref.next_ref = bf16[256,8192]{1,0:T(8,128)(2,1)} reshape(bf16[128,2,8192]{2,1,0:T(2,128)(2,1)} %param.10) | data formatting | bytes 8388608 | tf_op jit(solution)/shard_map/reshape | solution.py:347
  26.1 0.6 iota_convert_fusion
  26.6 0.1 copy.23
  26.8 0.1 copy.25
  26.9 0.1 copy.22
  27.0 0.1 copy.24
  27.1 0.0 copy-done.6
  27.2 1.1 tile.10
  28.3 0.3 slice.156
  28.6 0.2 reshape.96
  28.8 0.2 copy.26
  29.0 0.6 add_convert_fusion
  29.6 0.0 collective-permute-done
  29.7 1.6 collective-permute-start.1
  31.3 0.6 slice_bitcast_fusion.24
  31.9 0.6 slice_bitcast_fusion.9
  32.5 7.9 %collective-permute-done.1 = f32[2,4,2,19,128]{4,3,2,1,0:T(8,128)S(1)} collective-permute-done((f32[2,4,2,19,128]{4,3,2,1,0:T(8,128)S(1)}, f32[2,4,2,19,128]{4,3,2,1,0:T(8,128)S(1)}, u32[]{:S(2)}, u32[]{:S(2)}) %collective-permute-start.1) | collective-permute-done | bytes 155680 | tf_op jit(solution)/shard_map/ppermute | solution.py:30
  40.5 1.7 collective-permute-start.2
  42.2 0.0 collective-permute-done.4
  42.2 1.1 reshape.98.halo_ref
  43.3 12.6 %collective-permute-done.2 = f32[4,4,2,19,128]{4,3,2,1,0:T(8,128)S(1)} collective-permute-done((f32[4,4,2,19,128]{4,3,2,1,0:T(8,128)S(1)}, f32[4,4,2,19,128]{4,3,2,1,0:T(8,128)S(1)}, u32[]{:S(2)}, u32[]{:S(2)}) %collective-permute-start.2) | collective-permute-done | bytes 311328 | tf_op jit(solution)/shard_map/ppermute | solution.py:30
  55.9 0.1 pad_maximum_fusion.2
  56.0 0.4 copy.21
  56.4 1.6 collective-permute-start.3
  58.0 2.2 %copy-done = bf16[256,8192]{1,0:T(8,128)(2,1)S(1)} copy-done((bf16[256,8192]{1,0:T(8,128)(2,1)S(1)}, bf16[256,8192]{1,0:T(8,128)(2,1)}, u32[]{:S(2)}) %copy-start) | copy-done | bytes 4194328
  60.2 0.0 copy-start.8
  60.2 7.0 %front.1.polar_ref = bf16[256,4096]{1,0:T(8,128)(2,1)S(1)} custom-call(bf16[256,256]{1,0:T(8,128)(2,1)S(1)} %pad_maximum_fusion.5.steer_ref, bf16[768,256]{1,0:T(8,128)(2,1)S(1)} %bitcast.96, bf16[256,8192]{1,0:T(8,128)(2,1)S(1)} %copy-done, bf16[256,8192]{1,0:T(8,128)(2,1)S(1)} %copy-done, bf16[256,512]{1,0:T(8,128)(2,1)S(1)} %reshape.98.halo_ref), custom_call_target="tpu_custom_call" | custom-call | flops 8000000000 | bytes 7000000 | tf_op jit(solution)/shard_map/front/pallas_call | solution.py:65
  67.2 1.4 copy-done.5
  68.6 7.1 %collective-permute-done.3 = f32[8,4,2,19,128]{4,0,3,2,1:T(8,128)} collective-permute-done((f32[8,4,2,19,128]{4,0,3,2,1:T(8,128)S(1)}, f32[8,4,2,19,128]{4,0,3,2,1:T(8,128)}, u32[]{:S(2)}, u32[]{:S(2)}) %collective-permute-start.3) | collective-permute-done | bytes 622624 | tf_op jit(solution)/shard_map/ppermute | solution.py:30
  75.7 1.0 slice_bitcast_fusion.17
  76.7 0.1 concatenate.31
  76.8 0.9 slice_bitcast_fusion.2
  77.7 0.0 copy-done.10
  77.7 0.1 stack.22
  77.8 0.0 copy-done.7
  77.8 0.0 copy-done.8
  77.8 6.9 %fusion.2 = (f32[15,1,128,128]{3,2,1,0:T(8,128)S(1)}, f32[15,1,128,128]{3,2,1,0:T(8,128)S(1)}, f32[15,1,128,128]{3,2,1,0:T(8,128)S(1)}, f32[15,1,128,128]{3,2,1,0:T(8,128)S(1)}) fusion(f32[128]{0:T(128)S(1)} %copy-done.8, f32[15,128]{1,0:T(8,128)S(1)} %stack.22, f32[128]{0:T(128)S(1)} %copy-done.7), kind=kLoop, calls=%fused_computation.8 | loop fusion | flops 983040 | bytes 3940864 | tf_op jit(solution)/shard_map/cos | solution.py:345
  84.7 0.0 copy-start.2
  84.7 2.3 %pad_maximum_fusion = (f32[15,2,128,128]{3,2,1,0:T(8,128)}, f32[15,2,128,128]{3,2,1,0:T(8,128)}) fusion(f32[15,1,128,128]{3,2,1,0:T(8,128)S(1)} %get-tuple-element.45, f32[15,1,128,128]{3,2,1,0:T(8,128)S(1)} %get-tuple-element.46, f32[15,1,128,128]{3,2,1,0:T(8,128)S(1)} %get-tuple-element.42, f32[15,1,128,128]{3,2,1,0:T(8,128)S(1)} %get-tuple-element.41), kind=kLoop, calls=%fused_computation | loop fusion | flops 983040 | bytes 7864320 | tf_op jit(solution)/shard_map/stack | solution.py:343
  87.1 1.2 copy_dynamic-update-slice_fusion.data_ref
  88.3 4.4 %matrices.1 = (bf16[15,256,256]{2,1,0:T(8,128)(2,1)S(1)}, bf16[8,256,256]{2,1,0:T(8,128)(2,1)S(1)}) custom-call(s32[90]{0:T(128)S(1)} %copy-done.2, f32[16,4,2,19,128]{4,3,2,1,0:T(8,128)S(1)} %copy_dynamic-update-slice_fusion.data_ref), custom_call_target="tpu_custom_call" | custom-call | flops 5000000000 | bytes 5000000 | tf_op jit(solution)/shard_map/matrices/pallas_call | solution.py:140
  92.6 1.3 copy-done.4
  93.9 55.6 %tree.1.basis_ref = bf16[16,256,256]{2,1,0:T(8,128)(2,1)} custom-call(bf16[256,4096]{1,0:T(8,128)(2,1)} %copy-done.5, bf16[2,4096,256]{2,1,0:T(8,128)(2,1)} %map_ref.1, bf16[15,256,256]{2,1,0:T(8,128)(2,1)} %copy-done.4, bf16[8,256,256]{2,1,0:T(8,128)(2,1)S(1)} %get-tuple-element.8.own_ref, f32[15,2,128,128]{3,2,1,0:T(8,128)} %get-tuple-element.47.fine_ref, ...), custom_call_target="tpu_custom_call" | custom-call | flops 40000000000 | bytes 12000000 | tf_op jit(solution)/shard_map/tree/pallas_call | solution.py:217
  149.5 2.2 %copy-done.1 = bf16[256,2,32,128]{3,2,1,0:T(8,128)(2,1)S(1)} copy-done((bf16[256,2,32,128]{3,2,1,0:T(8,128)(2,1)S(1)}, bf16[256,2,32,128]{3,2,1,0:T(8,128)(2,1)}, u32[]{:S(2)}) %copy-start.1) | copy-done | bytes 4194328
  151.7 1.6 copy-done.3
  153.3 5.8 %tiles.1 = f32[32,2,32,256]{3,2,1,0:T(8,128)S(1)} custom-call(s32[1]{0:T(128)} %bitcast.place_ref, s32[256]{0:T(256)S(1)} %convert_element_type.66.cover_ref, bf16[16,256,256]{2,1,0:T(8,128)(2,1)S(1)} %copy-done.3, bf16[16,16,2,32,128]{4,3,2,1,0:T(8,128)(2,1)S(1)} %bitcast.97), custom_call_target="tpu_custom_call" | custom-call | flops 5000000000 | bytes 9000000 | tf_op jit(solution)/shard_map/tiles/pallas_call | solution.py:267
  159.1 0.1 fusion.5
  159.2 0.1 collective-permute-start.5
  159.3 1.9 %collective-permute-done.5 = bf16[16,2,32,256]{3,2,1,0:T(8,128)(2,1)S(1)} collective-permute-done((bf16[16,2,32,256]{3,2,1,0:T(8,128)(2,1)S(1)}, bf16[16,2,32,256]{3,2,1,0:T(8,128)(2,1)S(1)}, u32[]{:S(2)}, u32[]{:S(2)}) %collective-permute-start.5) | collective-permute-done | bytes 524320 | tf_op jit(solution)/shard_map/ppermute | solution.py:369
  161.1 0.2 fusion
  161.3 19.2 %all_to_all.5 = bf16[16,2,32,256]{3,2,1,0:T(8,128)(2,1)S(1)} all-to-all(bf16[16,2,32,256]{3,2,1,0:T(8,128)(2,1)S(1)} %fusion), channel_id=1, replica_groups=mesh['sub'=16,'rng'=2] {'sub'}, dimensions={0} | all-to-all | bytes 1048576 | tf_op jit(solution)/shard_map/all_to_all | solution.py:370
  180.5 0.7 convert_reduce_fusion
  (32 shorter events, 0.3 us)
Async XLA Ops:
  6.5 143.0 %all-gather.3.cloned.1.call-start = ((), (), s32[]{:S(2)}) async-start(), calls=%async_computation.1 | async-start | bytes 4456448 | tf_op jit(solution)/shard_map/all_gather | solution.py:329
  9.4 20.3 %collective-permute-start = (f32[1,4,2,19,128]{4,3,2,1,0:T(8,128)S(1)}, f32[1,4,2,19,128]{4,3,2,1,0:T(8,128)S(1)}, u32[]{:S(2)}, u32[]{:S(2)}) collective-permute-start(f32[1,4,2,19,128]{4,3,2,1,0:T(8,128)S(1)} %maximum_bitcast_fusion), channel_id=1, source_target_pairs={{0,16},{2,18},{4,20},{6,22},{8,24},{10,26},{12,28},{14,30},{16,0},... | collective-permute-start | bytes 233480 | tf_op jit(solution)/shard_map/ppermute | solution.py:30
  15.3 26.9 %collective-permute-start.4 = (bf16[128,2,512]{2,1,0:T(2,128)(2,1)}, bf16[128,2,512]{2,1,0:T(2,128)(2,1)}, u32[]{:S(2)}, u32[]{:S(2)}) collective-permute-start(bf16[128,2,512]{2,1,0:T(2,128)(2,1)} %slice.124), channel_id=1, source_target_pairs={{1,0},{3,2},{5,4},{7,6},{9,8},{11,10},{13,12},{15,14},{17,16},{19,... | collective-permute-start | bytes 786440 | tf_op jit(solution)/shard_map/ppermute | solution.py:24
  18.8 8.4 %copy-start.6 = (bf16[2,512]{1,0:T(2,128)(2,1)S(1)}, bf16[2,512]{1,0:T(2,128)(2,1)}, u32[]{:S(2)}) copy-start(bf16[2,512]{1,0:T(2,128)(2,1)} %param.11) | copy-start | bytes 6148
  29.7 10.8 %collective-permute-start.1 = (f32[2,4,2,19,128]{4,3,2,1,0:T(8,128)S(1)}, f32[2,4,2,19,128]{4,3,2,1,0:T(8,128)S(1)}, u32[]{:S(2)}, u32[]{:S(2)}) collective-permute-start(f32[2,4,2,19,128]{4,3,2,1,0:T(8,128)S(1)} %pad_maximum_fusion.4), channel_id=1, source_target_pairs={{0,8},{2,10},{4,12},{6,14},{8,0},{10,2},{12,4},{14,6},{16,24},{18,... | collective-permute-start | bytes 466952 | tf_op jit(solution)/shard_map/ppermute | solution.py:30
  40.5 15.5 %collective-permute-start.2 = (f32[4,4,2,19,128]{4,3,2,1,0:T(8,128)S(1)}, f32[4,4,2,19,128]{4,3,2,1,0:T(8,128)S(1)}, u32[]{:S(2)}, u32[]{:S(2)}) collective-permute-start(f32[4,4,2,19,128]{4,3,2,1,0:T(8,128)S(1)} %pad_maximum_fusion.3), channel_id=1, source_target_pairs={{0,4},{2,6},{4,0},{6,2},{8,12},{10,14},{12,8},{14,10},{16,20},{18,... | collective-permute-start | bytes 933896 | tf_op jit(solution)/shard_map/ppermute | solution.py:30
  56.4 19.4 %collective-permute-start.3 = (f32[8,4,2,19,128]{4,0,3,2,1:T(8,128)S(1)}, f32[8,4,2,19,128]{4,0,3,2,1:T(8,128)}, u32[]{:S(2)}, u32[]{:S(2)}) collective-permute-start(f32[8,4,2,19,128]{4,0,3,2,1:T(8,128)S(1)} %copy.21), channel_id=1, source_target_pairs={{0,2},{2,0},{4,6},{6,4},{8,10},{10,8},{12,14},{14,12},{16,18},{18,... | collective-permute-start | bytes 1867784 | tf_op jit(solution)/shard_map/ppermute | solution.py:30
  58.0 2.2 %copy-start = (bf16[256,8192]{1,0:T(8,128)(2,1)S(1)}, bf16[256,8192]{1,0:T(8,128)(2,1)}, u32[]{:S(2)}) copy-start(bf16[256,8192]{1,0:T(8,128)(2,1)} %reshape.97.raw_ref.next_ref) | copy-start | bytes 12582916
  60.2 16.6 %copy-start.9 = (f32[16]{0:T(128)S(1)}, f32[16]{0:T(128)}, u32[]{:S(2)}) copy-start(f32[16]{0:T(128)} %slice_bitcast_fusion.32) | copy-start | bytes 196
  60.2 16.6 %copy-start.11 = (f32[16]{0:T(128)S(1)}, f32[16]{0:T(128)}, u32[]{:S(2)}) copy-start(f32[16]{0:T(128)} %slice_bitcast_fusion.24) | copy-start | bytes 196
  60.2 17.5 %copy-start.10 = (f32[1,128]{1,0:T(1,128)S(1)}, f32[1,128]{1,0:T(1,128)}, u32[]{:S(2)}) copy-start(f32[1,128]{1,0:T(1,128)} %slice_bitcast_fusion.9) | copy-start | bytes 1540
  60.2 17.6 %copy-start.7 = (f32[128]{0:T(128)S(1)}, f32[128]{0:T(128)}, u32[]{:S(2)}) copy-start(f32[128]{0:T(128)} %iota_convert_fusion) | copy-start | bytes 1540
  60.2 17.6 %copy-start.8 = (f32[128]{0:T(128)S(1)}, f32[128]{0:T(128)}, u32[]{:S(2)}) copy-start(f32[128]{0:T(128)} %add_convert_fusion) | copy-start | bytes 1540
  67.2 1.4 copy-start.5
  84.7 3.6 %copy-start.2 = (s32[90]{0:T(128)S(1)}, s32[90]{0:T(128)}, u32[]{:S(2)}) copy-start(s32[90]{0:T(128)} %constant.63.pick_ref) | copy-start | bytes 1084
  92.6 1.3 copy-start.4
  149.5 2.2 %copy-start.1 = (bf16[256,2,32,128]{3,2,1,0:T(8,128)(2,1)S(1)}, bf16[256,2,32,128]{3,2,1,0:T(8,128)(2,1)}, u32[]{:S(2)}) copy-start(bf16[256,2,32,128]{3,2,1,0:T(8,128)(2,1)} %all-gather.3.cloned.1.call-done) | copy-start | bytes 12582916
  151.7 1.6 copy-start.3
  159.2 2.0 %collective-permute-start.5 = (bf16[16,2,32,256]{3,2,1,0:T(8,128)(2,1)S(1)}, bf16[16,2,32,256]{3,2,1,0:T(8,128)(2,1)S(1)}, u32[]{:S(2)}, u32[]{:S(2)}) collective-permute-start(bf16[16,2,32,256]{3,2,1,0:T(8,128)(2,1)S(1)} %fusion.5), channel_id=1, source_target_pairs={{0,1},{1,0},{2,3},{3,2},{4,5},{5,4},{6,7},{7,6},{8,9},{9,8},{10,11... | collective-permute-start | bytes 1572872 | tf_op jit(solution)/shard_map/ppermute | solution.py:369
Sparse Core Ops, SparseCore 0:
  16.8 79.9 all-gather.2
